TPU v7x, 256 devices: a whole 4x4x8 slice. The times are simulated.
256 devices in a mesh: row: 8 (over z), col: 8 (over x, core), rep: 4 (over y).
Axes of the slice: x: 4, y: 4, z: 8, core: 2. Of those that a mesh axis runs over, the one named last changes fastest.
Arguments:
- features: bfloat16 [65536, 256], P(('col', 'rep'), 'row'), may hold values from -6 to 6
- weight: bfloat16 [256, 256], replicated, may hold values from -0.375 to 0.375
- cotangent: bfloat16 [65536, 256], P(('row', 'col', 'rep')), may hold values from -6 to 6
- block_values: bfloat16 [8, 32, 320, 128, 128], P('row', ('col', 'rep')), may hold values from -0.0390625 to 0.0390625
- block_coords: int32 [8, 32, 320, 2], P('row', ('col', 'rep')), may hold values from 0 to 63, as said below
- block_counts: int32 [8, 32], P('row', ('col', 'rep')), may hold values from 1 to 320, as said below
Outputs:
- activations: bfloat16 [65536, 256], P(('row', 'col', 'rep'))
- input_grad: bfloat16 [65536, 256], P(('col', 'rep'), 'row')
- weight_grad: float32 [256, 256], replicated
Inputs may be any that keep to these rules, and one draw needn't show every extreme that they name: `block_coords`: each slot's row block is below 64 and its column block below 16. `block_counts`: some tile uses all 320 slots.
All inputs are finite; a program needn't handle non-finite values.
Results may differ from a plain program's by a relative error of at most 0.014.
Values may be sent and summed in bfloat16 or wider, within the bound.
No kernel may reach another device: no remote copies, remote signals or barrier semaphores. Data moves between devices by JAX's collectives and lax.ppermute only.
A program may use at most 128 MiB of HBM per device.

v0:
```python
import functools

import jax
import jax.numpy as jnp
from jax import lax
from jax.experimental import pallas as pl
from jax.experimental.pallas import tpu as pltpu
from jax.sharding import PartitionSpec as P

F32 = jnp.float32
BF16 = jnp.bfloat16
CORES = 2
UNROLL = 32
BIG = 44 << 20
VMEM = pl.BlockSpec(memory_space=pltpu.VMEM)
SMEM = pl.BlockSpec(memory_space=pltpu.SMEM)
HBM = pl.BlockSpec(memory_space=pltpu.HBM)


def call(kernel, args, out_shape, scratch=(), smem=0, hbm=0, limit=8 << 20, flops=0, aliases=None):
    moved = sum(a.size * a.dtype.itemsize for a in (*args, *out_shape))
    return pl.pallas_call(
        kernel,
        out_shape=out_shape,
        in_specs=[SMEM] * smem + [HBM] * hbm + [VMEM] * (len(args) - smem - hbm),
        out_specs=[VMEM] * len(out_shape),
        scratch_shapes=list(scratch),
        input_output_aliases=aliases or {},
        compiler_params=pltpu.CompilerParams(vmem_limit_bytes=limit),
        cost_estimate=pl.CostEstimate(flops=flops, bytes_accessed=moved, transcendentals=0),
    )(*args)


def shape(dims, dtype=BF16):
    return jax.ShapeDtypeStruct(dims, dtype)


def added(*arrays):
    total = arrays[0].astype(F32)
    for a in arrays[1:]:
        total = total + a.astype(F32)
    return total.astype(BF16)


def lanes(which, half):
    return pl.ds(pl.multiple_of(which * half, half), half)


def place(major, minor, core, block):
    return ((major * 4 + minor) * CORES + core) * 2 + block


PLACES = [(j, n, c, b) for j in range(4) for n in range(4) for c in range(CORES) for b in range(2)]


def block_copy(blocks_in, blocks, sems, t):
    part = pl.ds(t * UNROLL, UNROLL)
    return pltpu.make_async_copy(blocks_in.at[part], blocks.at[part], sems.at[t])


def forward_kernel(nz, pos_ref, col_ref, count_ref, at_ref, blocks_in, first, *refs):
    pieces, (send_a, send_b, keep_a, keep_b, blocks, turned, feat, acc, sems, first_sem) = refs[: nz - 1], refs[nz - 1 :]
    size = blocks.shape[1]
    turns = blocks.shape[0] // UNROLL
    shard = first.shape[0]
    half = acc.shape[2] // 2
    z, core = at_ref[0], at_ref[1]
    own = pltpu.make_async_copy(first, turned.at[pl.ds(pl.multiple_of(z * shard, shard), shard)], first_sem)
    own.start()
    for t in range(turns):
        block_copy(blocks_in, blocks, sems, t).start()
    rows = acc.shape[0] - 1

    def clear(r, carry):
        acc[r] = jnp.zeros(acc.shape[1:], F32)
        return carry

    lax.fori_loop(0, rows, clear, 0)
    for dz in range(1, nz):
        at = pl.multiple_of(lax.rem(z + dz, nz) * shard, shard)
        turned[pl.ds(at, shard), :] = pieces[dz - 1][...]
    own.wait()
    for c in range(feat.shape[0]):
        feat[c] = turned[:, c * size : (c + 1) * size].T
    count = count_ref[0]

    def turn(t, carry):
        block_copy(blocks_in, blocks, sems, t).wait()
        for u in range(UNROLL):
            s = t * UNROLL + u
            r = jnp.where(s < count, pos_ref[s], rows)
            acc[r] += jnp.dot(blocks[s], feat[col_ref[s]], preferred_element_type=F32)
        return carry

    lax.fori_loop(0, turns, turn, 0)
    for major, minor, c, b in PLACES:
        r = place(major, minor, c, b)
        for j, n, k, out_a, out_b, which in (
            (minor, major, 1 - c, send_a, send_b, 1 - core),
            (major, minor, c, keep_a, keep_b, core),
        ):
            value = acc[r, :, lanes(which, half)].astype(BF16)
            to = pl.ds((k * 2 + b) * size, size)
            if j == 2:
                out_a[n, to, :] = value
            else:
                out_b[(1, 3, 0).index(j), n, to, :] = value


def first_sum_kernel(keep_a, recv_a, passed_in, low, high, passed):
    low[...] = added(keep_a[:2], recv_a[:2])
    high[...] = added(keep_a[2:], recv_a[2:])


def second_sum_kernel(keep_b, recv_b, low, high, near_1, near_3):
    near_1[:2] = added(keep_b[0, :2], recv_b[0, :2], low[...])
    near_1[2:] = added(keep_b[0, 2:], recv_b[0, 2:])
    near_3[:2] = added(keep_b[1, :2], recv_b[1, :2])
    near_3[2:] = added(keep_b[1, 2:], recv_b[1, 2:], high[...])


def third_sum_kernel(keep_b, recv_b, minus, plus, *outs):
    for d in range(4):
        outs[d][...] = added(keep_b[2, d], recv_b[2, d], minus[d], plus[d])


def fourth_sum_kernel(a, b, c, d, own, send):
    rows = own.shape[0]
    own[...] = added(*(r[:rows] for r in (a, b, c, d)))
    send[...] = added(*(r[rows:] for r in (a, b, c, d)))


def middle_kernel(at_ref, own, other, weight, cotangent, act, back_own, send, w_keep, agg, back, terms):
    rows, half = own.shape
    core = at_ref[1]
    agg[:, lanes(core, half)] = own[...]
    agg[:, lanes(1 - core, half)] = other[...]
    pre = jnp.dot(agg[...], weight[...], preferred_element_type=F32)
    sigma = jax.nn.sigmoid(pre)
    grad = (cotangent[...].astype(F32) * sigma * (1.0 + pre * (1.0 - sigma))).astype(BF16)
    back[...] = lax.dot_general(
        grad, weight[...], (((1,), (1,)), ((), ())), preferred_element_type=F32
    ).astype(BF16)
    back_own[...] = back[:, lanes(core, half)]
    send[:rows, :] = back[:, lanes(1 - core, half)]
    act[...] = (pre * sigma).astype(BF16)
    terms[...] = lax.dot_general(
        agg[...], grad, (((0,), (0,)), ((), ())), preferred_element_type=F32
    )
    for k in range(2):
        columns = slice(k * half, (k + 1) * half)
        w_keep[k * half : (k + 1) * half, :] = terms[lanes(core, half), columns]
        send[rows + k * half : rows + (k + 1) * half, :] = terms[lanes(1 - core, half), columns].astype(BF16)


def in_order(table, first, *pieces):
    n = len(pieces)
    for d, piece in enumerate(pieces):
        table[lax.rem(first + d, n)] = piece.astype(F32)
    total = table[0]
    for d in range(1, n):
        total = total + table[d]
    return total


def pair_kernel(own, recv, w_keep, out):
    rows = own.shape[0]
    out[:rows, :] = own[...]
    out[rows : 2 * rows, :] = recv[:rows]
    out[2 * rows :, :] = added(w_keep[...], recv[rows:])


def line_kernel(at_ref, a, b, c, d, out, table):
    rows = table.shape[1] * 2
    for k, ref in enumerate((a, b, c, d)):
        out[k * rows : (k + 1) * rows, :] = ref[:rows]
    out[4 * rows :, :] = in_order(table, at_ref[3], *(ref[rows:] for ref in (a, b, c, d))).astype(BF16)


def halves_kernel(minus, plus, low, high):
    rows = high.shape[0]
    low[:rows, :] = minus[:rows]
    low[rows:, :] = minus[2 * rows :]
    high[...] = plus[rows : 2 * rows]


def plane_kernel(at_ref, own, plus, low, minus, out, table):
    rows = out.shape[0]
    out[...] = in_order(table, at_ref[2], *(ref[ref.shape[0] - rows :] for ref in (own, plus, low, minus))).astype(BF16)


def first_ring_kernel(up, up_term, down, down_term, w, w_recv, up_out, down_out):
    rows = up.shape[0]
    up_out[:rows, :] = added(up[...], up_term[...])
    down_out[:rows, :] = added(down[...], down_term[...])
    both = added(w[...], w_recv[...])
    up_out[rows:, :] = both
    down_out[rows:, :] = both


def second_ring_kernel(up, up_term, down, down_term, up_out, down_out):
    rows = up_term.shape[0]
    up_out[:rows, :] = added(up[:rows], up_term[...])
    up_out[rows:, :] = up[rows:]
    down_out[...] = added(down[:rows], down_term[...])


def third_ring_kernel(at_ref, up, up_term, down, own_term, w, w_plus, w_minus, up_out, own_out, w_out, table):
    rows = up_term.shape[0]
    up_out[...] = added(up[:rows], up_term[...])
    own_out[...] = down[...].astype(F32) + own_term[...].astype(F32)
    w_out[...] = in_order(table, lax.rem(at_ref[0], 4), *(ref[rows:] for ref in (w, w_plus, up, w_minus)))


def last_ring_kernel(at_ref, up, own, w, w_recv, out, w_out):
    total = added(up[...], own[...])
    width = total.shape[1]
    for c in range(out.shape[1] // width):
        out[:, c * width : (c + 1) * width] = total[c * out.shape[0] : (c + 1) * out.shape[0]]
    core, half = at_ref[1], w_out.shape[0] // 2
    for which, piece in ((core, w), (1 - core, w_recv)):
        for k in range(2):
            w_out[lanes(which, half), k * half : (k + 1) * half] = piece[k * half : (k + 1) * half]


def backward_kernel(nz, pos_ref, col_ref, count_ref, at_ref, blocks_in, *refs):
    mine, theirs, outs = refs[:5], refs[5:10], refs[10 : 10 + nz]
    blocks, back, acc, turned, sems = refs[10 + nz :]
    size = blocks.shape[1]
    turns = blocks.shape[0] // UNROLL
    half = back.shape[2] // 2
    z, core = at_ref[0], at_ref[1]
    for t in range(turns):
        block_copy(blocks_in, blocks, sems, t).start()
    for (own, minus, plus, low, high), is_mine in ((mine, True), (theirs, False)):
        for major, minor, c, b in PLACES:
            source = {0: own, 3: minus, 1: plus, 2: low if minor < 2 else high}[major]
            k = minor % 2 if major == 2 else minor
            k = ((k * CORES + c) * 2 + b) * size
            r = place(major, minor, c, b) if is_mine else place(minor, major, 1 - c, b)
            to = lanes(core if is_mine else 1 - core, half)
            back[r, :, to] = source[k : k + size, :]
    cols = acc.shape[0] - 1
    for c in range(cols):
        acc[c] = jnp.zeros(acc.shape[1:], F32)
    count = count_ref[0]

    def turn(t, carry):
        block_copy(blocks_in, blocks, sems, t).wait()
        for u in range(UNROLL):
            s = t * UNROLL + u
            c = jnp.where(s < count, col_ref[s], cols)
            acc[c] += lax.dot_general(
                blocks[s], back[pos_ref[s]], (((0,), (0,)), ((), ())), preferred_element_type=F32
            )
        return carry

    lax.fori_loop(0, turns, turn, 0)
    shard = turned.shape[1] // nz
    for c in range(cols):
        turned[c] = acc[c].astype(BF16).T
        for dz in range(nz):
            at = pl.multiple_of(lax.rem(z + dz, nz) * shard, shard)
            outs[dz][c * shard : (c + 1) * shard, :] = turned[c, pl.ds(at, shard), :]


def local(features, weight, cotangent, block_values, block_coords, block_counts):
    blocks, coords = block_values[0, 0], block_coords[0, 0]
    nz, ny = lax.axis_size("row"), lax.axis_size("rep")
    ncol = lax.axis_size("col")
    nx = ncol // CORES
    z, y = lax.axis_index("row"), lax.axis_index("rep")
    x, core = lax.axis_index("col") // CORES, lax.axis_index("col") % CORES
    at = jnp.stack([z, core, jnp.where(core == 0, x, y), jnp.where(core == 0, y, x)]).astype(jnp.int32)
    count = block_counts[0]
    slots, size, _ = blocks.shape
    rows_dev, width = cotangent.shape
    half = width // 2
    nodes, shard = features.shape
    flops = 2 * slots * size * size * width
    turns = slots // UNROLL

    def move(a, axis, d):
        pairs = []
        for i in range(nx):
            for c in range(CORES):
                for j in range(ny):
                    along_x = (axis == "major") == (c == 0)
                    to = ((i + d) % nx, j) if along_x else (i, (j + d) % ny)
                    pairs.append(((i * CORES + c) * ny + j, (to[0] * CORES + c) * ny + to[1]))
        return lax.ppermute(a, ("col", "rep"), pairs)

    def swap(a):
        return lax.ppermute(a, "col", [(i, i ^ 1) for i in range(ncol)])

    def along_z(a, d):
        return lax.ppermute(a, "row", [(i, (i + d) % nz) for i in range(nz)])

    def flip_z(a, bit):
        return lax.ppermute(a, "row", [(i, i ^ bit) for i in range(nz)])

    owner = coords[:, 0] // 2
    to_x = (owner // (ny * CORES) - x) % nx
    to_y = (owner % ny - y) % ny
    major, minor = jnp.where(core == 0, to_x, to_y), jnp.where(core == 0, to_y, to_x)
    pos = place(major, minor, (owner // ny) % CORES ^ core, coords[:, 0] % 2)
    col = coords[:, 1]

    shards = [None] * nz
    shards[0] = features.T
    for k in range(1, nz // 2 + 1):
        shards[nz - k] = along_z(shards[(nz - k + 1) % nz], 1)
        if k < nz // 2:
            shards[k] = along_z(shards[k - 1], -1)

    pair = CORES * rows_dev
    part_a, part_b = shape((4, pair, half)), shape((3, 4, pair, half))
    row_blocks = len(PLACES)
    send_a, send_b, keep_a, keep_b = call(
        functools.partial(forward_kernel, nz),
        (pos, col, count, at, blocks, *shards),
        [part_a, part_b, part_a, part_b],
        [
            pltpu.VMEM(blocks.shape, BF16),
            pltpu.VMEM((width, nodes), BF16),
            pltpu.VMEM((nodes // size, size, width), BF16),
            pltpu.VMEM((row_blocks + 1, size, width), F32),
            pltpu.SemaphoreType.DMA((turns,)),
            pltpu.SemaphoreType.DMA,
        ],
        smem=4,
        hbm=2,
        limit=BIG,
        flops=flops,
    )

    recv_a = swap(send_a)
    two, four, one = shape((2, pair, half)), shape((4, pair, half)), shape((pair, half))
    low, high, send_b = call(first_sum_kernel, (keep_a, recv_a, send_b), [two, two, part_b], aliases={2: 2})
    low, high, recv_b = move(low, "major", 1), move(high, "major", -1), swap(send_b)
    near_1, near_3 = call(second_sum_kernel, (keep_b, recv_b, low, high), [four] * 2)
    minus, plus = move(near_1, "major", 1), move(near_3, "major", -1)
    sums = call(third_sum_kernel, (keep_b, recv_b, minus, plus), [one] * 4)
    sums = [sums[0]] + [move(sums[d], "minor", d) for d in (1, 2, 3)]
    mine = shape((rows_dev, half))
    agg_own, agg_send = call(fourth_sum_kernel, sums, [mine] * 2)

    w_half = shape((width, half))
    activations, back_own, send, w_keep = call(
        middle_kernel,
        (at, agg_own, swap(agg_send), weight, cotangent),
        [shape((rows_dev, width)), mine, shape((rows_dev + width, half)), shape((width, half), F32)],
        [pltpu.VMEM((rows_dev, width), BF16)] * 2 + [pltpu.VMEM((width, width), F32)],
        smem=1,
    )
    table = pltpu.VMEM((4, width, half), F32)

    (base,) = call(pair_kernel, (back_own, swap(send), w_keep), [shape((pair + width, half))])
    near = [base] + [move(base, "minor", -d) for d in (1, 2, 3)]
    (line,) = call(line_kernel, (at, *near), [shape((4 * pair + width, half))], [table], smem=1)
    minus, plus = move(line, "major", 1), move(line, "major", -1)
    low, high = call(halves_kernel, (minus, plus), [shape((2 * pair + width, half)), shape((2 * pair, half))])
    low, high = move(low, "major", 1), move(high, "major", -1)
    rows_all = (line, minus, plus, low, high)
    (w,) = call(plane_kernel, (at, line, plus, low, minus), [w_half], [table], smem=1)

    ring, ring_w = shape((shard * nodes // size, size)), shape((shard * nodes // size + width, half))
    w_recv = flip_z(w, 4)
    terms = call(
        functools.partial(backward_kernel, nz),
        (pos, col, count, at, blocks, *rows_all, *(swap(a) for a in rows_all)),
        [ring] * nz,
        [
            pltpu.VMEM(blocks.shape, BF16),
            pltpu.VMEM((row_blocks, size, width), BF16),
            pltpu.VMEM((nodes // size + 1, size, width), F32),
            pltpu.VMEM((nodes // size, width, size), BF16),
            pltpu.SemaphoreType.DMA((turns,)),
        ],
        smem=4,
        hbm=1,
        limit=BIG,
        flops=flops,
    )
    up, down = along_z(terms[4], 1), along_z(terms[5], -1)
    own, down = call(first_ring_kernel, (up, terms[3], down, terms[6], w, w_recv), [ring_w] * 2)
    up, down = along_z(own, 1), along_z(down, -1)
    next_up, next_down = call(second_ring_kernel, (up, terms[2], down, terms[7]), [ring_w, ring])
    third_up, third_down = along_z(next_up, 1), along_z(next_down, -1)
    up, own, w = call(
        third_ring_kernel,
        (at, third_up, terms[1], third_down, terms[0], own, down, up),
        [ring, shape(ring.shape, F32), shape((width, half), F32)],
        [table],
        smem=1,
    )
    input_grad, weight_grad = call(
        last_ring_kernel,
        (at, along_z(up, 1), own, w, swap(w)),
        [shape((shard, nodes)), shape((width, width), F32)],
        smem=1,
    )
    return activations, input_grad.T, weight_grad


def solution(mesh):
    in_specs = (
        P(("col", "rep"), "row"),
        P(),
        P(("row", "col", "rep"), None),
        P("row", ("col", "rep"), None, None, None),
        P("row", ("col", "rep"), None, None),
        P("row", ("col", "rep")),
    )
    out_specs = (P(("row", "col", "rep"), None), P(("col", "rep"), "row"), P())
    return jax.shard_map(local, mesh=mesh, in_specs=in_specs, out_specs=out_specs, check_vma=False)
```

profile of v0, /device:TPU:8, one launch (start us, length us, event | category | flops | bytes accessed | tf_op | source)
XLA Modules:
  0.0 156.3 jit_solution(14091623329027536021)
XLA Ops:
  2.6 4.0 %collective-permute-start = (bf16[32,2048]{1,0:T(8,128)(2,1)}, bf16[32,2048]{1,0:T(8,128)(2,1)S(1)}, u32[]{:S(2)}, u32[]{:S(2)}) collective-permute-start(bf16[32,2048]{1,0:T(8,128)(2,1)} %bitcast.12), channel_id=1, source_target_pairs={{0,224},{32,0},{64,32},{96,64},{128,96},{160,128},{192,160},{224,1... | collective-permute-start | bytes 393224 | tf_op jit(solution)/shard_map/ppermute | solution.py:297
  6.7 3.6 %collective-permute-done.3.refs_6_ = bf16[32,2048]{1,0:T(8,128)(2,1)S(1)} collective-permute-done((bf16[32,2048]{1,0:T(8,128)(2,1)}, bf16[32,2048]{1,0:T(8,128)(2,1)S(1)}, u32[]{:S(2)}, u32[]{:S(2)}) %collective-permute-start.3) | collective-permute-done | bytes 131104 | tf_op jit(solution)/shard_map/ppermute | solution.py:297
  10.3 3.2 %collective-permute-start.1 = (bf16[32,2048]{1,0:T(8,128)(2,1)S(1)}, bf16[32,2048]{1,0:T(8,128)(2,1)S(1)}, u32[]{:S(2)}, u32[]{:S(2)}) collective-permute-start(bf16[32,2048]{1,0:T(8,128)(2,1)S(1)} %collective-permute-done.refs_0_), channel_id=1, source_target_pairs={{0,224},{32,0},{64,32},{96,64},{128,96},{160,128},{192,160},{224,1... | collective-permute-start | bytes 393224 | tf_op jit(solution)/shard_map/ppermute | solution.py:297
  13.5 2.9 %collective-permute-done.4.refs_5_ = bf16[32,2048]{1,0:T(8,128)(2,1)S(1)} collective-permute-done((bf16[32,2048]{1,0:T(8,128)(2,1)S(1)}, bf16[32,2048]{1,0:T(8,128)(2,1)S(1)}, u32[]{:S(2)}, u32[]{:S(2)}) %collective-permute-start.4) | collective-permute-done | bytes 131104 | tf_op jit(solution)/shard_map/ppermute | solution.py:297
  17.2 3.3 %collective-permute-start.2 = (bf16[32,2048]{1,0:T(8,128)(2,1)S(1)}, bf16[32,2048]{1,0:T(8,128)(2,1)S(1)}, u32[]{:S(2)}, u32[]{:S(2)}) collective-permute-start(bf16[32,2048]{1,0:T(8,128)(2,1)S(1)} %collective-permute-done.1.refs_1_), channel_id=1, source_target_pairs={{0,224},{32,0},{64,32},{96,64},{128,96},{160,128},{192,160},{224,1... | collective-permute-start | bytes 393224 | tf_op jit(solution)/shard_map/ppermute | solution.py:297
  23.4 5.4 %collective-permute-done.6.refs_3_ = bf16[32,2048]{1,0:T(8,128)(2,1)S(1)} collective-permute-done((bf16[32,2048]{1,0:T(8,128)(2,1)S(1)}, bf16[32,2048]{1,0:T(8,128)(2,1)S(1)}, u32[]{:S(2)}, u32[]{:S(2)}) %collective-permute-start.6) | collective-permute-done | bytes 131104 | tf_op jit(solution)/shard_map/ppermute | solution.py:297
  29.7 9.7 %shard_map.85 = (bf16[4,512,128]{2,1,0:T(8,128)(2,1)S(1)}, bf16[3,4,512,128]{3,2,1,0:T(8,128)(2,1)S(1)}, bf16[4,512,128]{2,1,0:T(8,128)(2,1)S(1)}, bf16[3,4,512,128]{3,2,1,0:T(8,128)(2,1)S(1)}) custom-call(s32[320]{0:T(512)S(1)} %fusion.9.pos_ref, s32[320]{0:T(512)S(1)} %get-tuple-element.79.col_ref, s32[1]{0:T(128)} %bitcast.9.count_ref, ...), custom_call_target="tpu_custom_call" | custom-call | flops 2684354560 | bytes 15731220 | tf_op jit(solution)/shard_map/pallas_call | solution.py:22
  45.1 4.3 %collective-permute-done.9.low = bf16[2,512,128]{2,1,0:T(8,128)(2,1)S(1)} collective-permute-done((bf16[2,512,128]{2,1,0:T(8,128)(2,1)S(1)}, bf16[2,512,128]{2,1,0:T(8,128)(2,1)S(1)}, u32[]{:S(2)}, u32[]{:S(2)}) %collective-permute-start.9) | collective-permute-done | bytes 262176 | tf_op jit(solution)/shard_map/ppermute | solution.py:291
  53.3 7.2 %collective-permute-done.11.minus = bf16[4,512,128]{2,1,0:T(8,128)(2,1)S(1)} collective-permute-done((bf16[4,512,128]{2,1,0:T(8,128)(2,1)S(1)}, bf16[4,512,128]{2,1,0:T(8,128)(2,1)S(1)}, u32[]{:S(2)}, u32[]{:S(2)}) %collective-permute-start.11) | collective-permute-done | bytes 524320 | tf_op jit(solution)/shard_map/ppermute | solution.py:291
  66.3 3.2 %collective-permute-done.14.c = bf16[512,128]{1,0:T(8,128)(2,1)S(1)} collective-permute-done((bf16[512,128]{1,0:T(8,128)(2,1)S(1)}, bf16[512,128]{1,0:T(8,128)(2,1)S(1)}, u32[]{:S(2)}, u32[]{:S(2)}) %collective-permute-start.14) | collective-permute-done | bytes 131104 | tf_op jit(solution)/shard_map/ppermute | solution.py:291
  80.2 2.8 %collective-permute-done.19.c = bf16[768,128]{1,0:T(8,128)(2,1)S(1)} collective-permute-done((bf16[768,128]{1,0:T(8,128)(2,1)S(1)}, bf16[768,128]{1,0:T(8,128)(2,1)S(1)}, u32[]{:S(2)}, u32[]{:S(2)}) %collective-permute-start.19) | collective-permute-done | bytes 196640 | tf_op jit(solution)/shard_map/ppermute | solution.py:291
  85.6 3.0 %collective-permute-start.22 = (bf16[2304,128]{1,0:T(8,128)(2,1)S(1)}, bf16[2304,128]{1,0:T(8,128)(2,1)S(1)}, u32[]{:S(2)}, u32[]{:S(2)}) collective-permute-start(bf16[2304,128]{1,0:T(8,128)(2,1)S(1)} %shard_map.92.refs_0_.own), channel_id=1, source_target_pairs={{0,24},{1,25},{2,26},{3,27},{4,7},{5,4},{6,5},{7,6},{8,0},{9,1},{1... | collective-permute-start | bytes 1769480 | tf_op jit(solution)/shard_map/ppermute | solution.py:291
  88.6 7.4 %collective-permute-done.22.plus.refs_2_ = bf16[2304,128]{1,0:T(8,128)(2,1)S(1)} collective-permute-done((bf16[2304,128]{1,0:T(8,128)(2,1)S(1)}, bf16[2304,128]{1,0:T(8,128)(2,1)S(1)}, u32[]{:S(2)}, u32[]{:S(2)}) %collective-permute-start.22) | collective-permute-done | bytes 589856 | tf_op jit(solution)/shard_map/ppermute | solution.py:291
  96.0 3.7 %collective-permute-done.21.minus.refs_1_ = bf16[2304,128]{1,0:T(8,128)(2,1)S(1)} collective-permute-done((bf16[2304,128]{1,0:T(8,128)(2,1)S(1)}, bf16[2304,128]{1,0:T(8,128)(2,1)S(1)}, u32[]{:S(2)}, u32[]{:S(2)}) %collective-permute-start.21) | collective-permute-done | bytes 589856 | tf_op jit(solution)/shard_map/ppermute | solution.py:291
  100.6 3.0 %collective-permute-start.24 = (bf16[1024,128]{1,0:T(8,128)(2,1)S(1)}, bf16[1024,128]{1,0:T(8,128)(2,1)S(1)}, u32[]{:S(2)}, u32[]{:S(2)}) collective-permute-start(bf16[1024,128]{1,0:T(8,128)(2,1)S(1)} %get-tuple-element.61), channel_id=1, source_target_pairs={{0,24},{1,25},{2,26},{3,27},{4,7},{5,4},{6,5},{7,6},{8,0},{9,1},{1... | collective-permute-start | bytes 786440 | tf_op jit(solution)/shard_map/ppermute | solution.py:291
  103.6 4.5 %collective-permute-done.23.refs_3_.low = bf16[1280,128]{1,0:T(8,128)(2,1)S(1)} collective-permute-done((bf16[1280,128]{1,0:T(8,128)(2,1)S(1)}, bf16[1280,128]{1,0:T(8,128)(2,1)S(1)}, u32[]{:S(2)}, u32[]{:S(2)}) %collective-permute-start.23) | collective-permute-done | bytes 327712 | tf_op jit(solution)/shard_map/ppermute | solution.py:291
  110.2 9.8 %shard_map.94 = (bf16[512,128]{1,0:T(8,128)(2,1)S(1)}, bf16[512,128]{1,0:T(8,128)(2,1)S(1)}, bf16[512,128]{1,0:T(8,128)(2,1)S(1)}, bf16[512,128]{1,0:T(8,128)(2,...) custom-call(s32[320]{0:T(512)S(1)} %fusion.9.pos_ref, ...), custom_call_target="tpu_custom_call" | custom-call | flops 2684354560 | bytes 16255508 | tf_op jit(solution)/shard_map/pallas_call | solution.py:22
  120.1 3.2 %collective-permute-start.31 = (bf16[512,128]{1,0:T(8,128)(2,1)S(1)}, bf16[512,128]{1,0:T(8,128)(2,1)S(1)}, u32[]{:S(2)}, u32[]{:S(2)}) collective-permute-start(bf16[512,128]{1,0:T(8,128)(2,1)S(1)} %get-tuple-element.64), channel_id=1, source_target_pairs={{0,224},{32,0},{64,32},{96,64},{128,96},{160,128},{192,160},{224,1... | collective-permute-start | bytes 393224 | tf_op jit(solution)/shard_map/ppermute | solution.py:297
  123.9 4.4 %collective-permute-start.32 = (bf16[256,128]{1,0:T(8,128)(2,1)S(1)}, bf16[256,128]{1,0:T(8,128)(2,1)S(1)}, u32[]{:S(2)}, u32[]{:S(2)}) collective-permute-start(bf16[256,128]{1,0:T(8,128)(2,1)S(1)} %shard_map.95.w), channel_id=1, source_target_pairs={{0,128},{32,160},{64,192},{96,224},{128,0},{160,32},{192,64},{224,... | collective-permute-start | bytes 196616 | tf_op jit(solution)/shard_map/ppermute | solution.py:300
  128.3 3.9 %collective-permute-done.32.w_recv = bf16[256,128]{1,0:T(8,128)(2,1)S(1)} collective-permute-done((bf16[256,128]{1,0:T(8,128)(2,1)S(1)}, bf16[256,128]{1,0:T(8,128)(2,1)S(1)}, u32[]{:S(2)}, u32[]{:S(2)}) %collective-permute-start.32) | collective-permute-done | bytes 65568 | tf_op jit(solution)/shard_map/ppermute | solution.py:300
  134.4 3.8 %collective-permute-done.34.down.w_plus = bf16[768,128]{1,0:T(8,128)(2,1)S(1)} collective-permute-done((bf16[768,128]{1,0:T(8,128)(2,1)S(1)}, bf16[768,128]{1,0:T(8,128)(2,1)S(1)}, u32[]{:S(2)}, u32[]{:S(2)}) %collective-permute-start.34) | collective-permute-done | bytes 196640 | tf_op jit(solution)/shard_map/ppermute | solution.py:297
  138.2 2.8 %collective-permute-done.33.up.w_minus = bf16[768,128]{1,0:T(8,128)(2,1)S(1)} collective-permute-done((bf16[768,128]{1,0:T(8,128)(2,1)S(1)}, bf16[768,128]{1,0:T(8,128)(2,1)S(1)}, u32[]{:S(2)}, u32[]{:S(2)}) %collective-permute-start.33) | collective-permute-done | bytes 196640 | tf_op jit(solution)/shard_map/ppermute | solution.py:297
  141.1 3.2 %collective-permute-start.36 = (bf16[512,128]{1,0:T(8,128)(2,1)S(1)}, bf16[512,128]{1,0:T(8,128)(2,1)S(1)}, u32[]{:S(2)}, u32[]{:S(2)}) collective-permute-start(bf16[512,128]{1,0:T(8,128)(2,1)S(1)} %get-tuple-element.72), channel_id=1, source_target_pairs={{0,224},{32,0},{64,32},{96,64},{128,96},{160,128},{192,160},{224,1... | collective-permute-start | bytes 393224 | tf_op jit(solution)/shard_map/ppermute | solution.py:297
  148.9 6.1 %collective-permute-done.37.up = bf16[512,128]{1,0:T(8,128)(2,1)S(1)} collective-permute-done((bf16[512,128]{1,0:T(8,128)(2,1)S(1)}, bf16[512,128]{1,0:T(8,128)(2,1)S(1)}, u32[]{:S(2)}, u32[]{:S(2)}) %collective-permute-start.37) | collective-permute-done | bytes 131104 | tf_op jit(solution)/shard_map/ppermute | solution.py:297
  (78 shorter events, 46.2 us)
Async XLA Ops:
  0.6 9.6 %collective-permute-start.3 = (bf16[32,2048]{1,0:T(8,128)(2,1)}, bf16[32,2048]{1,0:T(8,128)(2,1)S(1)}, u32[]{:S(2)}, u32[]{:S(2)}) collective-permute-start(bf16[32,2048]{1,0:T(8,128)(2,1)} %bitcast.11), channel_id=1, source_target_pairs={{0,32},{32,64},{64,96},{96,128},{128,160},{160,192},{192,224},{224... | collective-permute-start | bytes 393224 | tf_op jit(solution)/shard_map/ppermute | solution.py:297
  2.6 7.7 %collective-permute-start = (bf16[32,2048]{1,0:T(8,128)(2,1)}, bf16[32,2048]{1,0:T(8,128)(2,1)S(1)}, u32[]{:S(2)}, u32[]{:S(2)}) collective-permute-start(bf16[32,2048]{1,0:T(8,128)(2,1)} %bitcast.12), channel_id=1, source_target_pairs={{0,224},{32,0},{64,32},{96,64},{128,96},{160,128},{192,160},{224,1... | collective-permute-start | bytes 393224 | tf_op jit(solution)/shard_map/ppermute | solution.py:297
  10.3 7.0 %collective-permute-start.1 = (bf16[32,2048]{1,0:T(8,128)(2,1)S(1)}, bf16[32,2048]{1,0:T(8,128)(2,1)S(1)}, u32[]{:S(2)}, u32[]{:S(2)}) collective-permute-start(bf16[32,2048]{1,0:T(8,128)(2,1)S(1)} %collective-permute-done.refs_0_), channel_id=1, source_target_pairs={{0,224},{32,0},{64,32},{96,64},{128,96},{160,128},{192,160},{224,1... | collective-permute-start | bytes 393224 | tf_op jit(solution)/shard_map/ppermute | solution.py:297
  41.6 8.1 %collective-permute-start.8 = (bf16[3,4,512,128]{3,2,1,0:T(8,128)(2,1)S(1)}, bf16[3,4,512,128]{3,2,1,0:T(8,128)(2,1)S(1)}, u32[]{:S(2)}, u32[]{:S(2)}) collective-permute-start(bf16[3,4,512,128]{3,2,1,0:T(8,128)(2,1)S(1)} %get-tuple-element.45), channel_id=1, source_target_pairs={{0,4},{4,0},{8,12},{12,8},{16,20},{20,16},{24,28},{28,24},{1,5},{5... | collective-permute-start | bytes 4718600 | tf_op jit(solution)/shard_map/ppermute | solution.py:294
  41.8 7.6 %collective-permute-start.9 = (bf16[2,512,128]{2,1,0:T(8,128)(2,1)S(1)}, bf16[2,512,128]{2,1,0:T(8,128)(2,1)S(1)}, u32[]{:S(2)}, u32[]{:S(2)}) collective-permute-start(bf16[2,512,128]{2,1,0:T(8,128)(2,1)S(1)} %get-tuple-element.46), channel_id=1, source_target_pairs={{0,8},{1,9},{2,10},{3,11},{4,5},{5,6},{6,7},{7,4},{8,16},{9,17},{1... | collective-permute-start | bytes 786440 | tf_op jit(solution)/shard_map/ppermute | solution.py:291
  43.3 6.4 %collective-permute-start.10 = (bf16[2,512,128]{2,1,0:T(8,128)(2,1)S(1)}, bf16[2,512,128]{2,1,0:T(8,128)(2,1)S(1)}, u32[]{:S(2)}, u32[]{:S(2)}) collective-permute-start(bf16[2,512,128]{2,1,0:T(8,128)(2,1)S(1)} %get-tuple-element.47), channel_id=1, source_target_pairs={{0,24},{1,25},{2,26},{3,27},{4,7},{5,4},{6,5},{7,6},{8,0},{9,1},{1... | collective-permute-start | bytes 786440 | tf_op jit(solution)/shard_map/ppermute | solution.py:291
  50.0 10.5 %collective-permute-start.11 = (bf16[4,512,128]{2,1,0:T(8,128)(2,1)S(1)}, bf16[4,512,128]{2,1,0:T(8,128)(2,1)S(1)}, u32[]{:S(2)}, u32[]{:S(2)}) collective-permute-start(bf16[4,512,128]{2,1,0:T(8,128)(2,1)S(1)} %get-tuple-element.48), channel_id=1, source_target_pairs={{0,8},{1,9},{2,10},{3,11},{4,5},{5,6},{6,7},{7,4},{8,16},{9,17},{1... | collective-permute-start | bytes 1572872 | tf_op jit(solution)/shard_map/ppermute | solution.py:291
  51.6 9.2 %collective-permute-start.12 = (bf16[4,512,128]{2,1,0:T(8,128)(2,1)S(1)}, bf16[4,512,128]{2,1,0:T(8,128)(2,1)S(1)}, u32[]{:S(2)}, u32[]{:S(2)}) collective-permute-start(bf16[4,512,128]{2,1,0:T(8,128)(2,1)S(1)} %get-tuple-element.49), channel_id=1, source_target_pairs={{0,24},{1,25},{2,26},{3,27},{4,7},{5,4},{6,5},{7,6},{8,0},{9,1},{1... | collective-permute-start | bytes 1572872 | tf_op jit(solution)/shard_map/ppermute | solution.py:291
  62.9 6.6 %collective-permute-start.14 = (bf16[512,128]{1,0:T(8,128)(2,1)S(1)}, bf16[512,128]{1,0:T(8,128)(2,1)S(1)}, u32[]{:S(2)}, u32[]{:S(2)}) collective-permute-start(bf16[512,128]{1,0:T(8,128)(2,1)S(1)} %get-tuple-element.52), channel_id=1, source_target_pairs={{0,2},{1,3},{2,0},{3,1},{4,20},{5,21},{6,22},{7,23},{8,10},{9,11},... | collective-permute-start | bytes 393224 | tf_op jit(solution)/shard_map/ppermute | solution.py:291
  63.8 6.4 %collective-permute-start.15 = (bf16[512,128]{1,0:T(8,128)(2,1)S(1)}, bf16[512,128]{1,0:T(8,128)(2,1)S(1)}, u32[]{:S(2)}, u32[]{:S(2)}) collective-permute-start(bf16[512,128]{1,0:T(8,128)(2,1)S(1)} %get-tuple-element.53), channel_id=1, source_target_pairs={{0,3},{1,0},{2,1},{3,2},{4,28},{5,29},{6,30},{7,31},{8,11},{9,8},{... | collective-permute-start | bytes 393224 | tf_op jit(solution)/shard_map/ppermute | solution.py:291
  75.7 7.3 %collective-permute-start.19 = (bf16[768,128]{1,0:T(8,128)(2,1)S(1)}, bf16[768,128]{1,0:T(8,128)(2,1)S(1)}, u32[]{:S(2)}, u32[]{:S(2)}) collective-permute-start(bf16[768,128]{1,0:T(8,128)(2,1)S(1)} %shard_map.91.a), channel_id=1, source_target_pairs={{0,2},{1,3},{2,0},{3,1},{4,20},{5,21},{6,22},{7,23},{8,10},{9,11},... | collective-permute-start | bytes 589832 | tf_op jit(solution)/shard_map/ppermute | solution.py:291
  77.6 7.4 %collective-permute-start.18 = (bf16[768,128]{1,0:T(8,128)(2,1)S(1)}, bf16[768,128]{1,0:T(8,128)(2,1)S(1)}, u32[]{:S(2)}, u32[]{:S(2)}) collective-permute-start(bf16[768,128]{1,0:T(8,128)(2,1)S(1)} %shard_map.91.a), channel_id=1, source_target_pairs={{0,3},{1,0},{2,1},{3,2},{4,28},{5,29},{6,30},{7,31},{8,11},{9,8},{... | collective-permute-start | bytes 589832 | tf_op jit(solution)/shard_map/ppermute | solution.py:291
  85.6 10.4 %collective-permute-start.22 = (bf16[2304,128]{1,0:T(8,128)(2,1)S(1)}, bf16[2304,128]{1,0:T(8,128)(2,1)S(1)}, u32[]{:S(2)}, u32[]{:S(2)}) collective-permute-start(bf16[2304,128]{1,0:T(8,128)(2,1)S(1)} %shard_map.92.refs_0_.own), channel_id=1, source_target_pairs={{0,24},{1,25},{2,26},{3,27},{4,7},{5,4},{6,5},{7,6},{8,0},{9,1},{1... | collective-permute-start | bytes 1769480 | tf_op jit(solution)/shard_map/ppermute | solution.py:291
  88.6 11.1 %collective-permute-start.21 = (bf16[2304,128]{1,0:T(8,128)(2,1)S(1)}, bf16[2304,128]{1,0:T(8,128)(2,1)S(1)}, u32[]{:S(2)}, u32[]{:S(2)}) collective-permute-start(bf16[2304,128]{1,0:T(8,128)(2,1)S(1)} %shard_map.92.refs_0_.own), channel_id=1, source_target_pairs={{0,8},{1,9},{2,10},{3,11},{4,5},{5,6},{6,7},{7,4},{8,16},{9,17},{1... | collective-permute-start | bytes 1769480 | tf_op jit(solution)/shard_map/ppermute | solution.py:291
  99.8 8.4 %collective-permute-start.23 = (bf16[1280,128]{1,0:T(8,128)(2,1)S(1)}, bf16[1280,128]{1,0:T(8,128)(2,1)S(1)}, u32[]{:S(2)}, u32[]{:S(2)}) collective-permute-start(bf16[1280,128]{1,0:T(8,128)(2,1)S(1)} %get-tuple-element.60), channel_id=1, source_target_pairs={{0,8},{1,9},{2,10},{3,11},{4,5},{5,6},{6,7},{7,4},{8,16},{9,17},{1... | collective-permute-start | bytes 983048 | tf_op jit(solution)/shard_map/ppermute | solution.py:291
  99.9 8.8 %collective-permute-start.25 = (bf16[2304,128]{1,0:T(8,128)(2,1)S(1)}, bf16[2304,128]{1,0:T(8,128)(2,1)S(1)}, u32[]{:S(2)}, u32[]{:S(2)}) collective-permute-start(bf16[2304,128]{1,0:T(8,128)(2,1)S(1)} %shard_map.92.refs_0_.own), channel_id=1, source_target_pairs={{0,4},{4,0},{8,12},{12,8},{16,20},{20,16},{24,28},{28,24},{1,5},{5... | collective-permute-start | bytes 1769480 | tf_op jit(solution)/shard_map/ppermute | solution.py:294
  100.0 10.2 %collective-permute-start.27 = (bf16[2304,128]{1,0:T(8,128)(2,1)S(1)}, bf16[2304,128]{1,0:T(8,128)(2,1)S(1)}, u32[]{:S(2)}, u32[]{:S(2)}) collective-permute-start(bf16[2304,128]{1,0:T(8,128)(2,1)S(1)} %collective-permute-done.22.plus.refs_2_), channel_id=1, source_target_pairs={{0,4},{4,0},{8,12},{12,8},{16,20},{20,16},{24,28},{28,24},{1,5},{5... | collective-permute-start | bytes 1769480 | tf_op jit(solution)/shard_map/ppermute | solution.py:294
  100.5 9.7 %collective-permute-start.26 = (bf16[2304,128]{1,0:T(8,128)(2,1)S(1)}, bf16[2304,128]{1,0:T(8,128)(2,1)S(1)}, u32[]{:S(2)}, u32[]{:S(2)}) collective-permute-start(bf16[2304,128]{1,0:T(8,128)(2,1)S(1)} %collective-permute-done.21.minus.refs_1_), channel_id=1, source_target_pairs={{0,4},{4,0},{8,12},{12,8},{16,20},{20,16},{24,28},{28,24},{1,5},{5... | collective-permute-start | bytes 1769480 | tf_op jit(solution)/shard_map/ppermute | solution.py:294
  100.6 7.6 %collective-permute-start.24 = (bf16[1024,128]{1,0:T(8,128)(2,1)S(1)}, bf16[1024,128]{1,0:T(8,128)(2,1)S(1)}, u32[]{:S(2)}, u32[]{:S(2)}) collective-permute-start(bf16[1024,128]{1,0:T(8,128)(2,1)S(1)} %get-tuple-element.61), channel_id=1, source_target_pairs={{0,24},{1,25},{2,26},{3,27},{4,7},{5,4},{6,5},{7,6},{8,0},{9,1},{1... | collective-permute-start | bytes 786440 | tf_op jit(solution)/shard_map/ppermute | solution.py:291
  120.0 12.2 %collective-permute-start.30 = (bf16[512,128]{1,0:T(8,128)(2,1)S(1)}, bf16[512,128]{1,0:T(8,128)(2,1)S(1)}, u32[]{:S(2)}, u32[]{:S(2)}) collective-permute-start(bf16[512,128]{1,0:T(8,128)(2,1)S(1)} %get-tuple-element.62), channel_id=1, source_target_pairs={{0,32},{32,64},{64,96},{96,128},{128,160},{160,192},{192,224},{224... | collective-permute-start | bytes 393224 | tf_op jit(solution)/shard_map/ppermute | solution.py:297
  120.1 12.1 %collective-permute-start.31 = (bf16[512,128]{1,0:T(8,128)(2,1)S(1)}, bf16[512,128]{1,0:T(8,128)(2,1)S(1)}, u32[]{:S(2)}, u32[]{:S(2)}) collective-permute-start(bf16[512,128]{1,0:T(8,128)(2,1)S(1)} %get-tuple-element.64), channel_id=1, source_target_pairs={{0,224},{32,0},{64,32},{96,64},{128,96},{160,128},{192,160},{224,1... | collective-permute-start | bytes 393224 | tf_op jit(solution)/shard_map/ppermute | solution.py:297
  123.9 8.3 %collective-permute-start.32 = (bf16[256,128]{1,0:T(8,128)(2,1)S(1)}, bf16[256,128]{1,0:T(8,128)(2,1)S(1)}, u32[]{:S(2)}, u32[]{:S(2)}) collective-permute-start(bf16[256,128]{1,0:T(8,128)(2,1)S(1)} %shard_map.95.w), channel_id=1, source_target_pairs={{0,128},{32,160},{64,192},{96,224},{128,0},{160,32},{192,64},{224,... | collective-permute-start | bytes 196616 | tf_op jit(solution)/shard_map/ppermute | solution.py:300
  134.1 6.9 %collective-permute-start.33 = (bf16[768,128]{1,0:T(8,128)(2,1)S(1)}, bf16[768,128]{1,0:T(8,128)(2,1)S(1)}, u32[]{:S(2)}, u32[]{:S(2)}) collective-permute-start(bf16[768,128]{1,0:T(8,128)(2,1)S(1)} %get-tuple-element.66.w), channel_id=1, source_target_pairs={{0,32},{32,64},{64,96},{96,128},{128,160},{160,192},{192,224},{224... | collective-permute-start | bytes 589832 | tf_op jit(solution)/shard_map/ppermute | solution.py:297
  141.0 7.0 %collective-permute-start.35 = (bf16[768,128]{1,0:T(8,128)(2,1)S(1)}, bf16[768,128]{1,0:T(8,128)(2,1)S(1)}, u32[]{:S(2)}, u32[]{:S(2)}) collective-permute-start(bf16[768,128]{1,0:T(8,128)(2,1)S(1)} %get-tuple-element.70), channel_id=1, source_target_pairs={{0,32},{32,64},{64,96},{96,128},{128,160},{160,192},{192,224},{224... | collective-permute-start | bytes 589832 | tf_op jit(solution)/shard_map/ppermute | solution.py:297
  (18 other events, 109.4 us)
where the time goes:
time: 156 us
  waiting for transfers between devices  77.1 us (49%)
  starting transfers between devices  50.6 us (32%)
  Pallas kernels  25.3 us (16%)
  local copies, waits for them, and re-layouts  1.69 us (1%)
    ppermute x14, waiting for transfers between devices, move(): return lax.ppermute(a, ('col', 'rep'), pairs)  37.1 us
    ppermute x14, waiting for transfers between devices, along_z(): return lax.ppermute(a, 'row', [(i, (i + d) % nz) for i in range(nz)])  30.3 us
    pallas_call x15, Pallas kernels, call(): pl.pallas_call(kernel, out_shape=out_shape, in_specs=[SMEM] * smem + [HBM...  25.3 us
    ppermute x14, starting transfers between devices, move(): return lax.ppermute(a, ('col', 'rep'), pairs)  23 us
    ppermute x14, starting transfers between devices, along_z(): return lax.ppermute(a, 'row', [(i, (i + d) % nz) for i in range(nz)])  21.4 us
    ppermute x10, waiting for transfers between devices, swap(): return lax.ppermute(a, 'col', [(i, i ^ 1) for i in range(ncol)])  5.83 us
    ppermute x1, starting transfers between devices, flip_z(): return lax.ppermute(a, 'row', [(i, i ^ bit) for i in range(nz)])  4.38 us
    ppermute x1, waiting for transfers between devices, flip_z(): return lax.ppermute(a, 'row', [(i, i ^ bit) for i in range(nz)])  3.88 us
  transfers between devices with their start and end apart: 39, of which 26 were waited for; matrix products, arithmetic and copies ran while one was open for 1% of the time, Pallas kernels for 0%

commit v1 on v0

--- a/solution.py
+++ b/solution.py
@@ -10,7 +10,7 @@
 F32 = jnp.float32
 BF16 = jnp.bfloat16
 CORES = 2
-UNROLL = 32
+UNROLL = 64
 BIG = 44 << 20
 VMEM = pl.BlockSpec(memory_space=pltpu.VMEM)
 SMEM = pl.BlockSpec(memory_space=pltpu.SMEM)
@@ -53,20 +53,34 @@
 PLACES = [(j, n, c, b) for j in range(4) for n in range(4) for c in range(CORES) for b in range(2)]
 
 
+def row_place(coord_ref, at_ref, s):
+    r = coord_ref[0, s]
+    core, axes = at_ref[1], (at_ref[2], at_ref[3])
+    along_x, along_y = jnp.right_shift(r, 4), jnp.bitwise_and(jnp.right_shift(r, 1), 3)
+    major = jnp.bitwise_and(jnp.where(core == 0, along_x, along_y) - axes[0], 3)
+    minor = jnp.bitwise_and(jnp.where(core == 0, along_y, along_x) - axes[1], 3)
+    own = jnp.bitwise_xor(jnp.bitwise_and(jnp.right_shift(r, 3), 1), core)
+    return place(major, minor, own, jnp.bitwise_and(r, 1))
+
+
+def own_kernel(first, out, sem):
+    copy = pltpu.make_async_copy(first, out, sem)
+    copy.start()
+    copy.wait()
+
+
 def block_copy(blocks_in, blocks, sems, t):
     part = pl.ds(t * UNROLL, UNROLL)
     return pltpu.make_async_copy(blocks_in.at[part], blocks.at[part], sems.at[t])
 
 
-def forward_kernel(nz, pos_ref, col_ref, count_ref, at_ref, blocks_in, first, *refs):
-    pieces, (send_a, send_b, keep_a, keep_b, blocks, turned, feat, acc, sems, first_sem) = refs[: nz - 1], refs[nz - 1 :]
+def forward_kernel(nz, coord_ref, count_ref, at_ref, blocks_in, *refs):
+    pieces, (send_a, send_b, keep_a, keep_b, blocks, turned, feat, acc, sems) = refs[:nz], refs[nz:]
     size = blocks.shape[1]
     turns = blocks.shape[0] // UNROLL
-    shard = first.shape[0]
+    shard = pieces[0].shape[0]
     half = acc.shape[2] // 2
     z, core = at_ref[0], at_ref[1]
-    own = pltpu.make_async_copy(first, turned.at[pl.ds(pl.multiple_of(z * shard, shard), shard)], first_sem)
-    own.start()
     for t in range(turns):
         block_copy(blocks_in, blocks, sems, t).start()
     rows = acc.shape[0] - 1
@@ -76,10 +90,9 @@
         return carry
 
     lax.fori_loop(0, rows, clear, 0)
-    for dz in range(1, nz):
+    for dz in range(nz):
         at = pl.multiple_of(lax.rem(z + dz, nz) * shard, shard)
-        turned[pl.ds(at, shard), :] = pieces[dz - 1][...]
-    own.wait()
+        turned[pl.ds(at, shard), :] = pieces[dz][...]
     for c in range(feat.shape[0]):
         feat[c] = turned[:, c * size : (c + 1) * size].T
     count = count_ref[0]
@@ -88,8 +101,8 @@
         block_copy(blocks_in, blocks, sems, t).wait()
         for u in range(UNROLL):
             s = t * UNROLL + u
-            r = jnp.where(s < count, pos_ref[s], rows)
-            acc[r] += jnp.dot(blocks[s], feat[col_ref[s]], preferred_element_type=F32)
+            r = jnp.where(s < count, row_place(coord_ref, at_ref, s), rows)
+            acc[r] += jnp.dot(blocks[s], feat[coord_ref[1, s]], preferred_element_type=F32)
         return carry
 
     lax.fori_loop(0, turns, turn, 0)
@@ -177,39 +190,30 @@
     out[4 * rows :, :] = in_order(table, at_ref[3], *(ref[rows:] for ref in (a, b, c, d))).astype(BF16)
 
 
-def halves_kernel(minus, plus, low, high):
+def halves_kernel(minus, plus, passed_in, low, high, between, passed):
     rows = high.shape[0]
     low[:rows, :] = minus[:rows]
     low[rows:, :] = minus[2 * rows :]
     high[...] = plus[rows : 2 * rows]
-
-
-def plane_kernel(at_ref, own, plus, low, minus, out, table):
-    rows = out.shape[0]
-    out[...] = in_order(table, at_ref[2], *(ref[ref.shape[0] - rows :] for ref in (own, plus, low, minus))).astype(BF16)
-
-
-def first_ring_kernel(up, up_term, down, down_term, w, w_recv, up_out, down_out):
-    rows = up.shape[0]
-    up_out[:rows, :] = added(up[...], up_term[...])
-    down_out[:rows, :] = added(down[...], down_term[...])
-    both = added(w[...], w_recv[...])
-    up_out[rows:, :] = both
-    down_out[rows:, :] = both
-
-
-def second_ring_kernel(up, up_term, down, down_term, up_out, down_out):
+    between[: 2 * rows, :] = minus[: 2 * rows]
+    between[2 * rows :, :] = plus[: 2 * rows]
+
+
+def ring_kernel(up, up_term, down, down_term, up_out, down_out):
     rows = up_term.shape[0]
-    up_out[:rows, :] = added(up[:rows], up_term[...])
-    up_out[rows:, :] = up[rows:]
-    down_out[...] = added(down[:rows], down_term[...])
-
-
-def third_ring_kernel(at_ref, up, up_term, down, own_term, w, w_plus, w_minus, up_out, own_out, w_out, table):
+    for got, term, out in ((up, up_term, up_out), (down, down_term, down_out)):
+        out[:rows, :] = added(got[:rows], term[...])
+        out[rows:, :] = got[rows:]
+
+
+def third_ring_kernel(at_ref, up, up_term, down, own_term, *refs):
+    w, opposite, up_1, down_1, up_2, down_2, up_out, own_out, w_out, table = refs
     rows = up_term.shape[0]
     up_out[...] = added(up[:rows], up_term[...])
-    own_out[...] = down[...].astype(F32) + own_term[...].astype(F32)
-    w_out[...] = in_order(table, lax.rem(at_ref[0], 4), *(ref[rows:] for ref in (w, w_plus, up, w_minus)))
+    own_out[...] = down[:rows].astype(F32) + own_term[...].astype(F32)
+    tails = (ref[rows:] for ref in (down_1, down_2, down))
+    after = (ref[rows:] for ref in (up, up_2, up_1))
+    w_out[...] = in_order(table, at_ref[0], w[...], *tails, opposite[...], *after)
 
 
 def last_ring_kernel(at_ref, up, own, w, w_recv, out, w_out):
@@ -223,9 +227,11 @@
             w_out[lanes(which, half), k * half : (k + 1) * half] = piece[k * half : (k + 1) * half]
 
 
-def backward_kernel(nz, pos_ref, col_ref, count_ref, at_ref, blocks_in, *refs):
-    mine, theirs, outs = refs[:5], refs[5:10], refs[10 : 10 + nz]
-    blocks, back, acc, turned, sems = refs[10 + nz :]
+def backward_kernel(nz, coord_ref, count_ref, at_ref, blocks_in, *refs):
+    mine, (line, between, low, high), (w, *outs) = refs[:5], refs[5:9], refs[9 : 10 + nz]
+    blocks, back, acc, turned, table, sems = refs[10 + nz :]
+    rows = between.shape[0] // 2
+    theirs = (line, between.at[:rows], between.at[rows:], low, high)
     size = blocks.shape[1]
     turns = blocks.shape[0] // UNROLL
     half = back.shape[2] // 2
@@ -249,13 +255,19 @@
         block_copy(blocks_in, blocks, sems, t).wait()
         for u in range(UNROLL):
             s = t * UNROLL + u
-            c = jnp.where(s < count, col_ref[s], cols)
+            c = jnp.where(s < count, coord_ref[1, s], cols)
             acc[c] += lax.dot_general(
-                blocks[s], back[pos_ref[s]], (((0,), (0,)), ((), ())), preferred_element_type=F32
+                blocks[s], back[row_place(coord_ref, at_ref, s)], (((0,), (0,)), ((), ())), preferred_element_type=F32
             )
         return carry
 
     lax.fori_loop(0, turns, turn, 0)
+    own, minus, plus, low, high = mine
+    rows = w.shape[0]
+    tails = (ref[ref.shape[0] - rows :] for ref in (own, plus, low, minus))
+    w[...] = in_order(table, at_ref[2], *tails).astype(BF16)
+    for out in (outs[4], outs[5]):
+        out[out.shape[0] - rows :, :] = w[...]
     shard = turned.shape[1] // nz
     for c in range(cols):
         turned[c] = acc[c].astype(BF16).T
@@ -273,6 +285,7 @@
     x, core = lax.axis_index("col") // CORES, lax.axis_index("col") % CORES
     at = jnp.stack([z, core, jnp.where(core == 0, x, y), jnp.where(core == 0, y, x)]).astype(jnp.int32)
     count = block_counts[0]
+    coords = coords.T
     slots, size, _ = blocks.shape
     rows_dev, width = cotangent.shape
     half = width // 2
@@ -299,13 +312,6 @@
     def flip_z(a, bit):
         return lax.ppermute(a, "row", [(i, i ^ bit) for i in range(nz)])
 
-    owner = coords[:, 0] // 2
-    to_x = (owner // (ny * CORES) - x) % nx
-    to_y = (owner % ny - y) % ny
-    major, minor = jnp.where(core == 0, to_x, to_y), jnp.where(core == 0, to_y, to_x)
-    pos = place(major, minor, (owner // ny) % CORES ^ core, coords[:, 0] % 2)
-    col = coords[:, 1]
-
     shards = [None] * nz
     shards[0] = features.T
     for k in range(1, nz // 2 + 1):
@@ -313,12 +319,15 @@
         if k < nz // 2:
             shards[k] = along_z(shards[k - 1], -1)
 
+    (shards[0],) = call(
+        own_kernel, (shards[0],), [shape((shard, nodes))], [pltpu.SemaphoreType.DMA], hbm=1
+    )
     pair = CORES * rows_dev
     part_a, part_b = shape((4, pair, half)), shape((3, 4, pair, half))
     row_blocks = len(PLACES)
     send_a, send_b, keep_a, keep_b = call(
         functools.partial(forward_kernel, nz),
-        (pos, col, count, at, blocks, *shards),
+        (coords, count, at, blocks, *shards),
         [part_a, part_b, part_a, part_b],
         [
             pltpu.VMEM(blocks.shape, BF16),
@@ -326,10 +335,9 @@
             pltpu.VMEM((nodes // size, size, width), BF16),
             pltpu.VMEM((row_blocks + 1, size, width), F32),
             pltpu.SemaphoreType.DMA((turns,)),
-            pltpu.SemaphoreType.DMA,
         ],
-        smem=4,
-        hbm=2,
+        smem=3,
+        hbm=1,
         limit=BIG,
         flops=flops,
     )
@@ -359,39 +367,50 @@
     near = [base] + [move(base, "minor", -d) for d in (1, 2, 3)]
     (line,) = call(line_kernel, (at, *near), [shape((4 * pair + width, half))], [table], smem=1)
     minus, plus = move(line, "major", 1), move(line, "major", -1)
-    low, high = call(halves_kernel, (minus, plus), [shape((2 * pair + width, half)), shape((2 * pair, half))])
-    low, high = move(low, "major", 1), move(high, "major", -1)
-    rows_all = (line, minus, plus, low, high)
-    (w,) = call(plane_kernel, (at, line, plus, low, minus), [w_half], [table], smem=1)
-
-    ring, ring_w = shape((shard * nodes // size, size)), shape((shard * nodes // size + width, half))
-    w_recv = flip_z(w, 4)
-    terms = call(
+    sibling_line = swap(line)
+    low, high, between, sibling_line = call(
+        halves_kernel,
+        (minus, plus, sibling_line),
+        [
+            shape((2 * pair + width, half)),
+            shape((2 * pair, half)),
+            shape((8 * pair, half)),
+            shape(line.shape),
+        ],
+        aliases={2: 3},
+    )
+    low, high, between = move(low, "major", 1), move(high, "major", -1), swap(between)
+    rows_all = (line, minus, plus, low, high, sibling_line, between, swap(low), swap(high))
+
+    cells = shard * nodes // size
+    ring, ring_w = shape((cells, size)), shape((cells + width, size))
+    w, *terms = call(
         functools.partial(backward_kernel, nz),
-        (pos, col, count, at, blocks, *rows_all, *(swap(a) for a in rows_all)),
-        [ring] * nz,
+        (coords, count, at, blocks, *rows_all),
+        [w_half] + [ring_w if k in (4, 5) else ring for k in range(nz)],
         [
             pltpu.VMEM(blocks.shape, BF16),
             pltpu.VMEM((row_blocks, size, width), BF16),
             pltpu.VMEM((nodes // size + 1, size, width), F32),
             pltpu.VMEM((nodes // size, width, size), BF16),
+            table,
             pltpu.SemaphoreType.DMA((turns,)),
         ],
-        smem=4,
+        smem=3,
         hbm=1,
         limit=BIG,
         flops=flops,
     )
-    up, down = along_z(terms[4], 1), along_z(terms[5], -1)
-    own, down = call(first_ring_kernel, (up, terms[3], down, terms[6], w, w_recv), [ring_w] * 2)
-    up, down = along_z(own, 1), along_z(down, -1)
-    next_up, next_down = call(second_ring_kernel, (up, terms[2], down, terms[7]), [ring_w, ring])
-    third_up, third_down = along_z(next_up, 1), along_z(next_down, -1)
+    up_1, down_1 = along_z(terms[4], 1), along_z(terms[5], -1)
+    up, down = call(ring_kernel, (up_1, terms[3], down_1, terms[6]), [ring_w] * 2)
+    up_2, down_2 = along_z(up, 1), along_z(down, -1)
+    up, down = call(ring_kernel, (up_2, terms[2], down_2, terms[7]), [ring_w] * 2)
+    up_3, down_3 = along_z(up, 1), along_z(down, -1)
     up, own, w = call(
         third_ring_kernel,
-        (at, third_up, terms[1], third_down, terms[0], own, down, up),
-        [ring, shape(ring.shape, F32), shape((width, half), F32)],
-        [table],
+        (at, up_3, terms[1], down_3, terms[0], w, flip_z(w, 4), up_1, down_1, up_2, down_2),
+        [ring, shape((cells, size), F32), shape((width, half), F32)],
+        [pltpu.VMEM((nz, width, half), F32)],
         smem=1,
     )
     input_grad, weight_grad = call(

time: 156 us -> 154 us (0.987)
  waiting for transfers between devices: 77.1 us -> 75.1 us
  starting transfers between devices: 50.6 us -> 52.5 us
  Pallas kernels: 25.3 us -> 23.6 us
    ppermute x14, waiting for transfers between devices: 30.3 us -> 27.7 us  [along_z(): return lax.ppermute(a, 'row', [(i, (i + d) % nz) for i in range(nz)])]
    ppermute x14, starting transfers between devices: 21.4 us -> 23.9 us  [along_z(): return lax.ppermute(a, 'row', [(i, (i + d) % nz) for i in range(nz)])]
    pallas_call x15, Pallas kernels: 25.3 us -> 23.6 us  [call(): pl.pallas_call(kernel, out_shape=out_shape, in_specs=[SMEM] * smem + [HBM...]
    ppermute x10 -> x9, waiting for transfers between devices: 5.83 us -> 5.83 us  [swap(): return lax.ppermute(a, 'col', [(i, i ^ 1) for i in range(ncol)])]
  transfers between devices with their start and end apart: 39 -> 38, of which waited for: 26 -> 24; matrix products, arithmetic and copies ran while one was open for 1% -> 0% of each run, Pallas kernels for 0% -> 0%
where the time goes in v1:
time: 154 us
  waiting for transfers between devices  75.1 us (49%)
  starting transfers between devices  52.5 us (34%)
  Pallas kernels  23.6 us (15%)
  local copies, waits for them, and re-layouts  1.6 us (1%)
    ppermute x14, waiting for transfers between devices, move(): return lax.ppermute(a, ('col', 'rep'), pairs)  37.6 us
    ppermute x14, waiting for transfers between devices, along_z(): return lax.ppermute(a, 'row', [(i, (i + d) % nz) for i in range(nz)])  27.7 us
    ppermute x14, starting transfers between devices, along_z(): return lax.ppermute(a, 'row', [(i, (i + d) % nz) for i in range(nz)])  23.9 us
    pallas_call x15, Pallas kernels, call(): pl.pallas_call(kernel, out_shape=out_shape, in_specs=[SMEM] * smem + [HBM...  23.6 us
    ppermute x14, starting transfers between devices, move(): return lax.ppermute(a, ('col', 'rep'), pairs)  23 us
    ppermute x9, waiting for transfers between devices, swap(): return lax.ppermute(a, 'col', [(i, i ^ 1) for i in range(ncol)])  5.83 us
    ppermute x1, starting transfers between devices, flip_z(): return lax.ppermute(a, 'row', [(i, i ^ bit) for i in range(nz)])  4.29 us
    ppermute x1, waiting for transfers between devices, flip_z(): return lax.ppermute(a, 'row', [(i, i ^ bit) for i in range(nz)])  3.99 us
  transfers between devices with their start and end apart: 38, of which 24 were waited for; matrix products, arithmetic and copies ran while one was open for 0% of the time, Pallas kernels for 0%

profile of v1, /device:TPU:8, one launch (start us, length us, event | category | flops | bytes accessed | tf_op | source)
XLA Modules:
  0.0 154.2 jit_solution(4955993699741546497)
XLA Ops:
  2.6 4.0 %collective-permute-start = (bf16[32,2048]{1,0:T(8,128)(2,1)}, bf16[32,2048]{1,0:T(8,128)(2,1)S(1)}, u32[]{:S(2)}, u32[]{:S(2)}) collective-permute-start(bf16[32,2048]{1,0:T(8,128)(2,1)} %bitcast.14), channel_id=1, source_target_pairs={{0,224},{32,0},{64,32},{96,64},{128,96},{160,128},{192,160},{224,1... | collective-permute-start | bytes 393224 | tf_op jit(solution)/shard_map/ppermute | solution.py:310
  6.7 3.6 %collective-permute-done.3.refs_7_ = bf16[32,2048]{1,0:T(8,128)(2,1)S(1)} collective-permute-done((bf16[32,2048]{1,0:T(8,128)(2,1)}, bf16[32,2048]{1,0:T(8,128)(2,1)S(1)}, u32[]{:S(2)}, u32[]{:S(2)}) %collective-permute-start.3) | collective-permute-done | bytes 131104 | tf_op jit(solution)/shard_map/ppermute | solution.py:310
  10.3 3.2 %collective-permute-start.1 = (bf16[32,2048]{1,0:T(8,128)(2,1)S(1)}, bf16[32,2048]{1,0:T(8,128)(2,1)S(1)}, u32[]{:S(2)}, u32[]{:S(2)}) collective-permute-start(bf16[32,2048]{1,0:T(8,128)(2,1)S(1)} %collective-permute-done.refs_1_), channel_id=1, source_target_pairs={{0,224},{32,0},{64,32},{96,64},{128,96},{160,128},{192,160},{224,1... | collective-permute-start | bytes 393224 | tf_op jit(solution)/shard_map/ppermute | solution.py:310
  13.5 2.9 %collective-permute-done.4.refs_6_ = bf16[32,2048]{1,0:T(8,128)(2,1)S(1)} collective-permute-done((bf16[32,2048]{1,0:T(8,128)(2,1)S(1)}, bf16[32,2048]{1,0:T(8,128)(2,1)S(1)}, u32[]{:S(2)}, u32[]{:S(2)}) %collective-permute-start.4) | collective-permute-done | bytes 131104 | tf_op jit(solution)/shard_map/ppermute | solution.py:310
  16.5 3.2 %collective-permute-start.2 = (bf16[32,2048]{1,0:T(8,128)(2,1)S(1)}, bf16[32,2048]{1,0:T(8,128)(2,1)S(1)}, u32[]{:S(2)}, u32[]{:S(2)}) collective-permute-start(bf16[32,2048]{1,0:T(8,128)(2,1)S(1)} %collective-permute-done.1.refs_2_), channel_id=1, source_target_pairs={{0,224},{32,0},{64,32},{96,64},{128,96},{160,128},{192,160},{224,1... | collective-permute-start | bytes 393224 | tf_op jit(solution)/shard_map/ppermute | solution.py:310
  19.7 2.9 %collective-permute-done.5.refs_5_ = bf16[32,2048]{1,0:T(8,128)(2,1)S(1)} collective-permute-done((bf16[32,2048]{1,0:T(8,128)(2,1)S(1)}, bf16[32,2048]{1,0:T(8,128)(2,1)S(1)}, u32[]{:S(2)}, u32[]{:S(2)}) %collective-permute-start.5) | collective-permute-done | bytes 131104 | tf_op jit(solution)/shard_map/ppermute | solution.py:310
  24.4 4.4 %collective-permute-done.6.refs_4_ = bf16[32,2048]{1,0:T(8,128)(2,1)S(1)} collective-permute-done((bf16[32,2048]{1,0:T(8,128)(2,1)S(1)}, bf16[32,2048]{1,0:T(8,128)(2,1)S(1)}, u32[]{:S(2)}, u32[]{:S(2)}) %collective-permute-start.6) | collective-permute-done | bytes 131104 | tf_op jit(solution)/shard_map/ppermute | solution.py:310
  29.5 9.1 %shard_map.86 = (bf16[4,512,128]{2,1,0:T(8,128)(2,1)S(1)}, bf16[3,4,512,128]{3,2,1,0:T(8,128)(2,1)S(1)}, bf16[4,512,128]{2,1,0:T(8,128)(2,1)S(1)}, bf16[3,4,512,128]{3,2,1,0:T(8,128)(2,1)S(1)}) custom-call(s32[2,320]{1,0:T(2,128)S(1)} %bitcast.16, s32[1]{0:T(128)} %bitcast.11.count_ref, s32[4]{0:T(128)S(1)} %pad_add_fusion.at_ref, ...), custom_call_target="tpu_custom_call" | custom-call | flops 2684354560 | bytes 15731220 | tf_op jit(solution)/shard_map/pallas_call | solution.py:22
  44.2 4.3 %collective-permute-done.9.low = bf16[2,512,128]{2,1,0:T(8,128)(2,1)S(1)} collective-permute-done((bf16[2,512,128]{2,1,0:T(8,128)(2,1)S(1)}, bf16[2,512,128]{2,1,0:T(8,128)(2,1)S(1)}, u32[]{:S(2)}, u32[]{:S(2)}) %collective-permute-start.9) | collective-permute-done | bytes 262176 | tf_op jit(solution)/shard_map/ppermute | solution.py:304
  52.4 7.1 %collective-permute-done.11.minus = bf16[4,512,128]{2,1,0:T(8,128)(2,1)S(1)} collective-permute-done((bf16[4,512,128]{2,1,0:T(8,128)(2,1)S(1)}, bf16[4,512,128]{2,1,0:T(8,128)(2,1)S(1)}, u32[]{:S(2)}, u32[]{:S(2)}) %collective-permute-start.11) | collective-permute-done | bytes 524320 | tf_op jit(solution)/shard_map/ppermute | solution.py:304
  65.2 3.2 %collective-permute-done.14.c = bf16[512,128]{1,0:T(8,128)(2,1)S(1)} collective-permute-done((bf16[512,128]{1,0:T(8,128)(2,1)S(1)}, bf16[512,128]{1,0:T(8,128)(2,1)S(1)}, u32[]{:S(2)}, u32[]{:S(2)}) %collective-permute-start.14) | collective-permute-done | bytes 131104 | tf_op jit(solution)/shard_map/ppermute | solution.py:304
  84.6 3.0 %collective-permute-start.22 = (bf16[2304,128]{1,0:T(8,128)(2,1)S(1)}, bf16[2304,128]{1,0:T(8,128)(2,1)S(1)}, u32[]{:S(2)}, u32[]{:S(2)}) collective-permute-start(bf16[2304,128]{1,0:T(8,128)(2,1)S(1)} %shard_map.93.refs_0_), channel_id=1, source_target_pairs={{0,24},{1,25},{2,26},{3,27},{4,7},{5,4},{6,5},{7,6},{8,0},{9,1},{1... | collective-permute-start | bytes 1769480 | tf_op jit(solution)/shard_map/ppermute | solution.py:304
  87.6 7.4 %collective-permute-done.22.plus.refs_2_ = bf16[2304,128]{1,0:T(8,128)(2,1)S(1)} collective-permute-done((bf16[2304,128]{1,0:T(8,128)(2,1)S(1)}, bf16[2304,128]{1,0:T(8,128)(2,1)S(1)}, u32[]{:S(2)}, u32[]{:S(2)}) %collective-permute-start.22) | collective-permute-done | bytes 589856 | tf_op jit(solution)/shard_map/ppermute | solution.py:304
  95.0 3.7 %collective-permute-done.21.minus.refs_1_ = bf16[2304,128]{1,0:T(8,128)(2,1)S(1)} collective-permute-done((bf16[2304,128]{1,0:T(8,128)(2,1)S(1)}, bf16[2304,128]{1,0:T(8,128)(2,1)S(1)}, u32[]{:S(2)}, u32[]{:S(2)}) %collective-permute-start.21) | collective-permute-done | bytes 589856 | tf_op jit(solution)/shard_map/ppermute | solution.py:304
  99.0 3.2 %collective-permute-start.25 = (bf16[1024,128]{1,0:T(8,128)(2,1)S(1)}, bf16[1024,128]{1,0:T(8,128)(2,1)S(1)}, u32[]{:S(2)}, u32[]{:S(2)}) collective-permute-start(bf16[1024,128]{1,0:T(8,128)(2,1)S(1)} %get-tuple-element.64), channel_id=1, source_target_pairs={{0,24},{1,25},{2,26},{3,27},{4,7},{5,4},{6,5},{7,6},{8,0},{9,1},{1... | collective-permute-start | bytes 786440 | tf_op jit(solution)/shard_map/ppermute | solution.py:304
  102.3 5.0 %collective-permute-done.24.refs_3_ = bf16[1280,128]{1,0:T(8,128)(2,1)S(1)} collective-permute-done((bf16[1280,128]{1,0:T(8,128)(2,1)S(1)}, bf16[1280,128]{1,0:T(8,128)(2,1)S(1)}, u32[]{:S(2)}, u32[]{:S(2)}) %collective-permute-start.24) | collective-permute-done | bytes 327712 | tf_op jit(solution)/shard_map/ppermute | solution.py:304
  109.3 9.2 %shard_map.95 = (bf16[256,128]{1,0:T(8,128)(2,1)S(1)}, bf16[512,128]{1,0:T(8,128)(2,1)S(1)}, bf16[512,128]{1,0:T(8,128)(2,1)S(1)}, bf16[512,128]{1,0:T(8,128)(2,...) custom-call(s32[2,320]{1,0:T(2,128)S(1)} %bitcast.17, ...), custom_call_target="tpu_custom_call" | custom-call | flops 2684354560 | bytes 16321044 | tf_op jit(solution)/shard_map/pallas_call | solution.py:22
  118.6 3.2 %collective-permute-start.30 = (bf16[768,128]{1,0:T(8,128)(2,1)S(1)}, bf16[768,128]{1,0:T(8,128)(2,1)S(1)}, u32[]{:S(2)}, u32[]{:S(2)}) collective-permute-start(bf16[768,128]{1,0:T(8,128)(2,1)S(1)} %get-tuple-element.69), channel_id=1, source_target_pairs={{0,224},{32,0},{64,32},{96,64},{128,96},{160,128},{192,160},{224,1... | collective-permute-start | bytes 589832 | tf_op jit(solution)/shard_map/ppermute | solution.py:310
  121.8 4.9 %collective-permute-done.29.up.refs_2_ = bf16[768,128]{1,0:T(8,128)(2,1)S(1)} collective-permute-done((bf16[768,128]{1,0:T(8,128)(2,1)S(1)}, bf16[768,128]{1,0:T(8,128)(2,1)S(1)}, u32[]{:S(2)}, u32[]{:S(2)}) %collective-permute-start.29) | collective-permute-done | bytes 196640 | tf_op jit(solution)/shard_map/ppermute | solution.py:310
  126.9 3.2 %collective-permute-start.32 = (bf16[768,128]{1,0:T(8,128)(2,1)S(1)}, bf16[768,128]{1,0:T(8,128)(2,1)S(1)}, u32[]{:S(2)}, u32[]{:S(2)}) collective-permute-start(bf16[768,128]{1,0:T(8,128)(2,1)S(1)} %get-tuple-element.73), channel_id=1, source_target_pairs={{0,224},{32,0},{64,32},{96,64},{128,96},{160,128},{192,160},{224,1... | collective-permute-start | bytes 589832 | tf_op jit(solution)/shard_map/ppermute | solution.py:310
  130.1 4.1 %collective-permute-done.31.up.refs_4_ = bf16[768,128]{1,0:T(8,128)(2,1)S(1)} collective-permute-done((bf16[768,128]{1,0:T(8,128)(2,1)S(1)}, bf16[768,128]{1,0:T(8,128)(2,1)S(1)}, u32[]{:S(2)}, u32[]{:S(2)}) %collective-permute-start.31) | collective-permute-done | bytes 196640 | tf_op jit(solution)/shard_map/ppermute | solution.py:310
  137.6 4.3 %collective-permute-start.35 = (bf16[256,128]{1,0:T(8,128)(2,1)S(1)}, bf16[256,128]{1,0:T(8,128)(2,1)S(1)}, u32[]{:S(2)}, u32[]{:S(2)}) collective-permute-start(bf16[256,128]{1,0:T(8,128)(2,1)S(1)} %get-tuple-element.79.refs_0_), channel_id=1, source_target_pairs={{0,128},{32,160},{64,192},{96,224},{128,0},{160,32},{192,64},{224,... | collective-permute-start | bytes 196616 | tf_op jit(solution)/shard_map/ppermute | solution.py:313
  141.9 4.0 %collective-permute-done.35.refs_1_ = bf16[256,128]{1,0:T(8,128)(2,1)S(1)} collective-permute-done((bf16[256,128]{1,0:T(8,128)(2,1)S(1)}, bf16[256,128]{1,0:T(8,128)(2,1)S(1)}, u32[]{:S(2)}, u32[]{:S(2)}) %collective-permute-start.35) | collective-permute-done | bytes 65568 | tf_op jit(solution)/shard_map/ppermute | solution.py:313
  148.1 4.8 %collective-permute-done.36.up = bf16[512,128]{1,0:T(8,128)(2,1)S(1)} collective-permute-done((bf16[512,128]{1,0:T(8,128)(2,1)S(1)}, bf16[512,128]{1,0:T(8,128)(2,1)S(1)}, u32[]{:S(2)}, u32[]{:S(2)}) %collective-permute-start.36) | collective-permute-done | bytes 131104 | tf_op jit(solution)/shard_map/ppermute | solution.py:310
  (76 shorter events, 44.6 us)
Async XLA Ops:
  0.6 9.6 %collective-permute-start.3 = (bf16[32,2048]{1,0:T(8,128)(2,1)}, bf16[32,2048]{1,0:T(8,128)(2,1)S(1)}, u32[]{:S(2)}, u32[]{:S(2)}) collective-permute-start(bf16[32,2048]{1,0:T(8,128)(2,1)} %bitcast.13), channel_id=1, source_target_pairs={{0,32},{32,64},{64,96},{96,128},{128,160},{160,192},{192,224},{224... | collective-permute-start | bytes 393224 | tf_op jit(solution)/shard_map/ppermute | solution.py:310
  2.6 7.7 %collective-permute-start = (bf16[32,2048]{1,0:T(8,128)(2,1)}, bf16[32,2048]{1,0:T(8,128)(2,1)S(1)}, u32[]{:S(2)}, u32[]{:S(2)}) collective-permute-start(bf16[32,2048]{1,0:T(8,128)(2,1)} %bitcast.14), channel_id=1, source_target_pairs={{0,224},{32,0},{64,32},{96,64},{128,96},{160,128},{192,160},{224,1... | collective-permute-start | bytes 393224 | tf_op jit(solution)/shard_map/ppermute | solution.py:310
  16.5 8.0 %collective-permute-start.2 = (bf16[32,2048]{1,0:T(8,128)(2,1)S(1)}, bf16[32,2048]{1,0:T(8,128)(2,1)S(1)}, u32[]{:S(2)}, u32[]{:S(2)}) collective-permute-start(bf16[32,2048]{1,0:T(8,128)(2,1)S(1)} %collective-permute-done.1.refs_2_), channel_id=1, source_target_pairs={{0,224},{32,0},{64,32},{96,64},{128,96},{160,128},{192,160},{224,1... | collective-permute-start | bytes 393224 | tf_op jit(solution)/shard_map/ppermute | solution.py:310
  40.7 8.1 %collective-permute-start.8 = (bf16[3,4,512,128]{3,2,1,0:T(8,128)(2,1)S(1)}, bf16[3,4,512,128]{3,2,1,0:T(8,128)(2,1)S(1)}, u32[]{:S(2)}, u32[]{:S(2)}) collective-permute-start(bf16[3,4,512,128]{3,2,1,0:T(8,128)(2,1)S(1)} %get-tuple-element.48), channel_id=1, source_target_pairs={{0,4},{4,0},{8,12},{12,8},{16,20},{20,16},{24,28},{28,24},{1,5},{5... | collective-permute-start | bytes 4718600 | tf_op jit(solution)/shard_map/ppermute | solution.py:307
  40.9 7.6 %collective-permute-start.9 = (bf16[2,512,128]{2,1,0:T(8,128)(2,1)S(1)}, bf16[2,512,128]{2,1,0:T(8,128)(2,1)S(1)}, u32[]{:S(2)}, u32[]{:S(2)}) collective-permute-start(bf16[2,512,128]{2,1,0:T(8,128)(2,1)S(1)} %get-tuple-element.49), channel_id=1, source_target_pairs={{0,8},{1,9},{2,10},{3,11},{4,5},{5,6},{6,7},{7,4},{8,16},{9,17},{1... | collective-permute-start | bytes 786440 | tf_op jit(solution)/shard_map/ppermute | solution.py:304
  42.4 6.4 %collective-permute-start.10 = (bf16[2,512,128]{2,1,0:T(8,128)(2,1)S(1)}, bf16[2,512,128]{2,1,0:T(8,128)(2,1)S(1)}, u32[]{:S(2)}, u32[]{:S(2)}) collective-permute-start(bf16[2,512,128]{2,1,0:T(8,128)(2,1)S(1)} %get-tuple-element.50), channel_id=1, source_target_pairs={{0,24},{1,25},{2,26},{3,27},{4,7},{5,4},{6,5},{7,6},{8,0},{9,1},{1... | collective-permute-start | bytes 786440 | tf_op jit(solution)/shard_map/ppermute | solution.py:304
  49.1 10.5 %collective-permute-start.11 = (bf16[4,512,128]{2,1,0:T(8,128)(2,1)S(1)}, bf16[4,512,128]{2,1,0:T(8,128)(2,1)S(1)}, u32[]{:S(2)}, u32[]{:S(2)}) collective-permute-start(bf16[4,512,128]{2,1,0:T(8,128)(2,1)S(1)} %get-tuple-element.51), channel_id=1, source_target_pairs={{0,8},{1,9},{2,10},{3,11},{4,5},{5,6},{6,7},{7,4},{8,16},{9,17},{1... | collective-permute-start | bytes 1572872 | tf_op jit(solution)/shard_map/ppermute | solution.py:304
  50.7 9.2 %collective-permute-start.12 = (bf16[4,512,128]{2,1,0:T(8,128)(2,1)S(1)}, bf16[4,512,128]{2,1,0:T(8,128)(2,1)S(1)}, u32[]{:S(2)}, u32[]{:S(2)}) collective-permute-start(bf16[4,512,128]{2,1,0:T(8,128)(2,1)S(1)} %get-tuple-element.52), channel_id=1, source_target_pairs={{0,24},{1,25},{2,26},{3,27},{4,7},{5,4},{6,5},{7,6},{8,0},{9,1},{1... | collective-permute-start | bytes 1572872 | tf_op jit(solution)/shard_map/ppermute | solution.py:304
  61.8 6.6 %collective-permute-start.14 = (bf16[512,128]{1,0:T(8,128)(2,1)S(1)}, bf16[512,128]{1,0:T(8,128)(2,1)S(1)}, u32[]{:S(2)}, u32[]{:S(2)}) collective-permute-start(bf16[512,128]{1,0:T(8,128)(2,1)S(1)} %get-tuple-element.55), channel_id=1, source_target_pairs={{0,2},{1,3},{2,0},{3,1},{4,20},{5,21},{6,22},{7,23},{8,10},{9,11},... | collective-permute-start | bytes 393224 | tf_op jit(solution)/shard_map/ppermute | solution.py:304
  62.7 6.4 %collective-permute-start.15 = (bf16[512,128]{1,0:T(8,128)(2,1)S(1)}, bf16[512,128]{1,0:T(8,128)(2,1)S(1)}, u32[]{:S(2)}, u32[]{:S(2)}) collective-permute-start(bf16[512,128]{1,0:T(8,128)(2,1)S(1)} %get-tuple-element.56), channel_id=1, source_target_pairs={{0,3},{1,0},{2,1},{3,2},{4,28},{5,29},{6,30},{7,31},{8,11},{9,8},{... | collective-permute-start | bytes 393224 | tf_op jit(solution)/shard_map/ppermute | solution.py:304
  74.6 7.3 %collective-permute-start.19 = (bf16[768,128]{1,0:T(8,128)(2,1)S(1)}, bf16[768,128]{1,0:T(8,128)(2,1)S(1)}, u32[]{:S(2)}, u32[]{:S(2)}) collective-permute-start(bf16[768,128]{1,0:T(8,128)(2,1)S(1)} %shard_map.92.a), channel_id=1, source_target_pairs={{0,2},{1,3},{2,0},{3,1},{4,20},{5,21},{6,22},{7,23},{8,10},{9,11},... | collective-permute-start | bytes 589832 | tf_op jit(solution)/shard_map/ppermute | solution.py:304
  76.5 7.4 %collective-permute-start.18 = (bf16[768,128]{1,0:T(8,128)(2,1)S(1)}, bf16[768,128]{1,0:T(8,128)(2,1)S(1)}, u32[]{:S(2)}, u32[]{:S(2)}) collective-permute-start(bf16[768,128]{1,0:T(8,128)(2,1)S(1)} %shard_map.92.a), channel_id=1, source_target_pairs={{0,3},{1,0},{2,1},{3,2},{4,28},{5,29},{6,30},{7,31},{8,11},{9,8},{... | collective-permute-start | bytes 589832 | tf_op jit(solution)/shard_map/ppermute | solution.py:304
  84.6 10.4 %collective-permute-start.22 = (bf16[2304,128]{1,0:T(8,128)(2,1)S(1)}, bf16[2304,128]{1,0:T(8,128)(2,1)S(1)}, u32[]{:S(2)}, u32[]{:S(2)}) collective-permute-start(bf16[2304,128]{1,0:T(8,128)(2,1)S(1)} %shard_map.93.refs_0_), channel_id=1, source_target_pairs={{0,24},{1,25},{2,26},{3,27},{4,7},{5,4},{6,5},{7,6},{8,0},{9,1},{1... | collective-permute-start | bytes 1769480 | tf_op jit(solution)/shard_map/ppermute | solution.py:304
  87.6 11.1 %collective-permute-start.21 = (bf16[2304,128]{1,0:T(8,128)(2,1)S(1)}, bf16[2304,128]{1,0:T(8,128)(2,1)S(1)}, u32[]{:S(2)}, u32[]{:S(2)}) collective-permute-start(bf16[2304,128]{1,0:T(8,128)(2,1)S(1)} %shard_map.93.refs_0_), channel_id=1, source_target_pairs={{0,8},{1,9},{2,10},{3,11},{4,5},{5,6},{6,7},{7,4},{8,16},{9,17},{1... | collective-permute-start | bytes 1769480 | tf_op jit(solution)/shard_map/ppermute | solution.py:304
  98.8 10.5 %collective-permute-start.26 = (bf16[4096,128]{1,0:T(8,128)(2,1)S(1)}, bf16[4096,128]{1,0:T(8,128)(2,1)S(1)}, u32[]{:S(2)}, u32[]{:S(2)}) collective-permute-start(bf16[4096,128]{1,0:T(8,128)(2,1)S(1)} %get-tuple-element.66), channel_id=1, source_target_pairs={{0,4},{4,0},{8,12},{12,8},{16,20},{20,16},{24,28},{28,24},{1,5},{5... | collective-permute-start | bytes 3145736 | tf_op jit(solution)/shard_map/ppermute | solution.py:307
  98.9 8.4 %collective-permute-start.24 = (bf16[1280,128]{1,0:T(8,128)(2,1)S(1)}, bf16[1280,128]{1,0:T(8,128)(2,1)S(1)}, u32[]{:S(2)}, u32[]{:S(2)}) collective-permute-start(bf16[1280,128]{1,0:T(8,128)(2,1)S(1)} %get-tuple-element.63), channel_id=1, source_target_pairs={{0,8},{1,9},{2,10},{3,11},{4,5},{5,6},{6,7},{7,4},{8,16},{9,17},{1... | collective-permute-start | bytes 983048 | tf_op jit(solution)/shard_map/ppermute | solution.py:304
  99.0 8.3 %collective-permute-start.25 = (bf16[1024,128]{1,0:T(8,128)(2,1)S(1)}, bf16[1024,128]{1,0:T(8,128)(2,1)S(1)}, u32[]{:S(2)}, u32[]{:S(2)}) collective-permute-start(bf16[1024,128]{1,0:T(8,128)(2,1)S(1)} %get-tuple-element.64), channel_id=1, source_target_pairs={{0,24},{1,25},{2,26},{3,27},{4,7},{5,4},{6,5},{7,6},{8,0},{9,1},{1... | collective-permute-start | bytes 786440 | tf_op jit(solution)/shard_map/ppermute | solution.py:304
  118.5 8.2 %collective-permute-start.29 = (bf16[768,128]{1,0:T(8,128)(2,1)S(1)}, bf16[768,128]{1,0:T(8,128)(2,1)S(1)}, u32[]{:S(2)}, u32[]{:S(2)}) collective-permute-start(bf16[768,128]{1,0:T(8,128)(2,1)S(1)} %get-tuple-element.67), channel_id=1, source_target_pairs={{0,32},{32,64},{64,96},{96,128},{128,160},{160,192},{192,224},{224... | collective-permute-start | bytes 589832 | tf_op jit(solution)/shard_map/ppermute | solution.py:310
  118.6 8.1 %collective-permute-start.30 = (bf16[768,128]{1,0:T(8,128)(2,1)S(1)}, bf16[768,128]{1,0:T(8,128)(2,1)S(1)}, u32[]{:S(2)}, u32[]{:S(2)}) collective-permute-start(bf16[768,128]{1,0:T(8,128)(2,1)S(1)} %get-tuple-element.69), channel_id=1, source_target_pairs={{0,224},{32,0},{64,32},{96,64},{128,96},{160,128},{192,160},{224,1... | collective-permute-start | bytes 589832 | tf_op jit(solution)/shard_map/ppermute | solution.py:310
  126.8 7.4 %collective-permute-start.31 = (bf16[768,128]{1,0:T(8,128)(2,1)S(1)}, bf16[768,128]{1,0:T(8,128)(2,1)S(1)}, u32[]{:S(2)}, u32[]{:S(2)}) collective-permute-start(bf16[768,128]{1,0:T(8,128)(2,1)S(1)} %get-tuple-element.71), channel_id=1, source_target_pairs={{0,32},{32,64},{64,96},{96,128},{128,160},{160,192},{192,224},{224... | collective-permute-start | bytes 589832 | tf_op jit(solution)/shard_map/ppermute | solution.py:310
  126.9 7.3 %collective-permute-start.32 = (bf16[768,128]{1,0:T(8,128)(2,1)S(1)}, bf16[768,128]{1,0:T(8,128)(2,1)S(1)}, u32[]{:S(2)}, u32[]{:S(2)}) collective-permute-start(bf16[768,128]{1,0:T(8,128)(2,1)S(1)} %get-tuple-element.73), channel_id=1, source_target_pairs={{0,224},{32,0},{64,32},{96,64},{128,96},{160,128},{192,160},{224,1... | collective-permute-start | bytes 589832 | tf_op jit(solution)/shard_map/ppermute | solution.py:310
  134.3 11.6 %collective-permute-start.33 = (bf16[768,128]{1,0:T(8,128)(2,1)S(1)}, bf16[768,128]{1,0:T(8,128)(2,1)S(1)}, u32[]{:S(2)}, u32[]{:S(2)}) collective-permute-start(bf16[768,128]{1,0:T(8,128)(2,1)S(1)} %get-tuple-element.75), channel_id=1, source_target_pairs={{0,32},{32,64},{64,96},{96,128},{128,160},{160,192},{192,224},{224... | collective-permute-start | bytes 589832 | tf_op jit(solution)/shard_map/ppermute | solution.py:310
  136.5 9.4 %collective-permute-start.34 = (bf16[768,128]{1,0:T(8,128)(2,1)S(1)}, bf16[768,128]{1,0:T(8,128)(2,1)S(1)}, u32[]{:S(2)}, u32[]{:S(2)}) collective-permute-start(bf16[768,128]{1,0:T(8,128)(2,1)S(1)} %get-tuple-element.77), channel_id=1, source_target_pairs={{0,224},{32,0},{64,32},{96,64},{128,96},{160,128},{192,160},{224,1... | collective-permute-start | bytes 589832 | tf_op jit(solution)/shard_map/ppermute | solution.py:310
  137.6 8.3 %collective-permute-start.35 = (bf16[256,128]{1,0:T(8,128)(2,1)S(1)}, bf16[256,128]{1,0:T(8,128)(2,1)S(1)}, u32[]{:S(2)}, u32[]{:S(2)}) collective-permute-start(bf16[256,128]{1,0:T(8,128)(2,1)S(1)} %get-tuple-element.79.refs_0_), channel_id=1, source_target_pairs={{0,128},{32,160},{64,192},{96,224},{128,0},{160,32},{192,64},{224,... | collective-permute-start | bytes 196616 | tf_op jit(solution)/shard_map/ppermute | solution.py:313
  (18 other events, 99.7 us)

commit v2 on v1

--- a/solution.py
+++ b/solution.py
@@ -160,10 +160,15 @@
     terms[...] = lax.dot_general(
         agg[...], grad, (((0,), (0,)), ((), ())), preferred_element_type=F32
     )
-    for k in range(2):
-        columns = slice(k * half, (k + 1) * half)
-        w_keep[k * half : (k + 1) * half, :] = terms[lanes(core, half), columns]
-        send[rows + k * half : rows + (k + 1) * half, :] = terms[lanes(1 - core, half), columns].astype(BF16)
+    step = half // 4
+    for n in range(4):
+        own_at = pl.multiple_of(core * half + lax.rem(at_ref[3] + n, 4) * step, step)
+        send_at = pl.multiple_of((1 - core) * half + lax.rem(at_ref[2] + n, 4) * step, step)
+        for k in range(2):
+            columns = slice(k * half, (k + 1) * half)
+            to = (n * 2 + k) * step
+            w_keep[to : to + step, :] = terms[pl.ds(own_at, step), columns]
+            send[rows + to : rows + to + step, :] = terms[pl.ds(send_at, step), columns].astype(BF16)
 
 
 def in_order(table, first, *pieces):
@@ -176,18 +181,20 @@
     return total
 
 
-def pair_kernel(own, recv, w_keep, out):
-    rows = own.shape[0]
-    out[:rows, :] = own[...]
-    out[rows : 2 * rows, :] = recv[:rows]
-    out[2 * rows :, :] = added(w_keep[...], recv[rows:])
-
-
-def line_kernel(at_ref, a, b, c, d, out, table):
-    rows = table.shape[1] * 2
+def pair_kernel(own, recv, w_keep, *outs):
+    rows, part = own.shape[0], w_keep.shape[0] // 4
+    for d, out in enumerate(outs):
+        n = (-d) % 4 * part
+        out[:rows, :] = own[...]
+        out[rows : 2 * rows, :] = recv[:rows]
+        out[2 * rows :, :] = added(w_keep[n : n + part], recv[rows + n : rows + n + part])
+
+
+def line_kernel(a, b, c, d, out):
+    whole = (out.shape[0] - a.shape[0]) // 3
     for k, ref in enumerate((a, b, c, d)):
-        out[k * rows : (k + 1) * rows, :] = ref[:rows]
-    out[4 * rows :, :] = in_order(table, at_ref[3], *(ref[rows:] for ref in (a, b, c, d))).astype(BF16)
+        out[k * whole : (k + 1) * whole, :] = ref[:whole]
+    out[4 * whole :, :] = added(*(ref[whole:] for ref in (a, b, c, d)))
 
 
 def halves_kernel(minus, plus, passed_in, low, high, between, passed):
@@ -216,15 +223,24 @@
     w_out[...] = in_order(table, at_ref[0], w[...], *tails, opposite[...], *after)
 
 
-def last_ring_kernel(at_ref, up, own, w, w_recv, out, w_out):
+def last_ring_kernel(at_ref, up, own, wa, wb, wc, wd, out, w_out):
     total = added(up[...], own[...])
     width = total.shape[1]
     for c in range(out.shape[1] // width):
         out[:, c * width : (c + 1) * width] = total[c * out.shape[0] : (c + 1) * out.shape[0]]
-    core, half = at_ref[1], w_out.shape[0] // 2
-    for which, piece in ((core, w), (1 - core, w_recv)):
-        for k in range(2):
-            w_out[lanes(which, half), k * half : (k + 1) * half] = piece[k * half : (k + 1) * half]
+    part = wa.shape[0]
+    for d, piece in enumerate((wa, wb, wc, wd)):
+        w_out[pl.ds(pl.multiple_of(lax.rem(at_ref[3] + d, 4) * part, part), part), :] = piece[...]
+
+
+def weight_kernel(at_ref, mine, theirs, out):
+    core, half = at_ref[1], out.shape[0] // 2
+    step = half // 4
+    for which, piece in ((core, mine), (1 - core, theirs)):
+        for n in range(4):
+            at = pl.ds(pl.multiple_of(which * half + n * step, step), step)
+            for k in range(2):
+                out[at, k * half : (k + 1) * half] = piece[(n * 2 + k) * step : (n * 2 + k + 1) * step]
 
 
 def backward_kernel(nz, coord_ref, count_ref, at_ref, blocks_in, *refs):
@@ -353,7 +369,7 @@
     mine = shape((rows_dev, half))
     agg_own, agg_send = call(fourth_sum_kernel, sums, [mine] * 2)
 
-    w_half = shape((width, half))
+    part = width // 4
     activations, back_own, send, w_keep = call(
         middle_kernel,
         (at, agg_own, swap(agg_send), weight, cotangent),
@@ -361,18 +377,17 @@
         [pltpu.VMEM((rows_dev, width), BF16)] * 2 + [pltpu.VMEM((width, width), F32)],
         smem=1,
     )
-    table = pltpu.VMEM((4, width, half), F32)
-
-    (base,) = call(pair_kernel, (back_own, swap(send), w_keep), [shape((pair + width, half))])
-    near = [base] + [move(base, "minor", -d) for d in (1, 2, 3)]
-    (line,) = call(line_kernel, (at, *near), [shape((4 * pair + width, half))], [table], smem=1)
+
+    near = call(pair_kernel, (back_own, swap(send), w_keep), [shape((pair + part, half))] * 4)
+    near = [near[0]] + [move(near[d], "minor", -d) for d in (1, 2, 3)]
+    (line,) = call(line_kernel, near, [shape((4 * pair + part, half))])
     minus, plus = move(line, "major", 1), move(line, "major", -1)
     sibling_line = swap(line)
     low, high, between, sibling_line = call(
         halves_kernel,
         (minus, plus, sibling_line),
         [
-            shape((2 * pair + width, half)),
+            shape((2 * pair + part, half)),
             shape((2 * pair, half)),
             shape((8 * pair, half)),
             shape(line.shape),
@@ -383,17 +398,17 @@
     rows_all = (line, minus, plus, low, high, sibling_line, between, swap(low), swap(high))
 
     cells = shard * nodes // size
-    ring, ring_w = shape((cells, size)), shape((cells + width, size))
+    ring, ring_w = shape((cells, size)), shape((cells + part, size))
     w, *terms = call(
         functools.partial(backward_kernel, nz),
         (coords, count, at, blocks, *rows_all),
-        [w_half] + [ring_w if k in (4, 5) else ring for k in range(nz)],
+        [shape((part, half))] + [ring_w if k in (4, 5) else ring for k in range(nz)],
         [
             pltpu.VMEM(blocks.shape, BF16),
             pltpu.VMEM((row_blocks, size, width), BF16),
             pltpu.VMEM((nodes // size + 1, size, width), F32),
             pltpu.VMEM((nodes // size, width, size), BF16),
-            table,
+            pltpu.VMEM((4, part, half), F32),
             pltpu.SemaphoreType.DMA((turns,)),
         ],
         smem=3,
@@ -409,16 +424,18 @@
     up, own, w = call(
         third_ring_kernel,
         (at, up_3, terms[1], down_3, terms[0], w, flip_z(w, 4), up_1, down_1, up_2, down_2),
-        [ring, shape((cells, size), F32), shape((width, half), F32)],
-        [pltpu.VMEM((nz, width, half), F32)],
+        [ring, shape((cells, size), F32), shape((part, half), F32)],
+        [pltpu.VMEM((nz, part, half), F32)],
         smem=1,
     )
-    input_grad, weight_grad = call(
+    w = [w] + [move(w, "minor", -d) for d in (1, 2, 3)]
+    input_grad, w = call(
         last_ring_kernel,
-        (at, along_z(up, 1), own, w, swap(w)),
-        [shape((shard, nodes)), shape((width, width), F32)],
+        (at, along_z(up, 1), own, *w),
+        [shape((shard, nodes)), shape((width, half), F32)],
         smem=1,
     )
+    (weight_grad,) = call(weight_kernel, (at, w, swap(w)), [shape((width, width), F32)], smem=1)
     return activations, input_grad.T, weight_grad
 
 

time: 154 us -> 156 us (1.013)
  waiting for transfers between devices: 75.1 us -> 69.2 us
  starting transfers between devices: 52.5 us -> 58.3 us
    ppermute x14, waiting for transfers between devices: 27.7 us -> 20.9 us  [along_z(): return lax.ppermute(a, 'row', [(i, (i + d) % nz) for i in range(nz)])]
    ppermute x14 -> x17, starting transfers between devices: 23 us -> 28.1 us  [move(): return lax.ppermute(a, ('col', 'rep'), pairs)]
    pallas_call x15 -> x16, Pallas kernels: 23.6 us -> 24.1 us  [call(): pl.pallas_call(kernel, out_shape=out_shape, in_specs=[SMEM] * smem + [HBM...]
    ppermute x14 -> x17, waiting for transfers between devices: 37.6 us -> 37.9 us  [move(): return lax.ppermute(a, ('col', 'rep'), pairs)]
  transfers between devices with their start and end apart: 38 -> 41, of which waited for: 24 -> 26; matrix products, arithmetic and copies ran while one was open for 0% -> 0% of each run, Pallas kernels for 0% -> 0%
where the time goes in v2:
time: 156 us; the launch traced here: 155 us
  waiting for transfers between devices  69.2 us (44%)
  starting transfers between devices  58.3 us (37%)
  Pallas kernels  24.1 us (15%)
  local copies, waits for them, and re-layouts  1.6 us (1%)
    ppermute x17, waiting for transfers between devices, move(): return lax.ppermute(a, ('col', 'rep'), pairs)  37.9 us
    ppermute x17, starting transfers between devices, move(): return lax.ppermute(a, ('col', 'rep'), pairs)  28.1 us
    pallas_call x16, Pallas kernels, call(): pl.pallas_call(kernel, out_shape=out_shape, in_specs=[SMEM] * smem + [HBM...  24.1 us
    ppermute x14, starting transfers between devices, along_z(): return lax.ppermute(a, 'row', [(i, (i + d) % nz) for i in range(nz)])  23.8 us
    ppermute x14, waiting for transfers between devices, along_z(): return lax.ppermute(a, 'row', [(i, (i + d) % nz) for i in range(nz)])  20.9 us
    ppermute x9, waiting for transfers between devices, swap(): return lax.ppermute(a, 'col', [(i, i ^ 1) for i in range(ncol)])  7.1 us
    ppermute x1, starting transfers between devices, flip_z(): return lax.ppermute(a, 'row', [(i, i ^ bit) for i in range(nz)])  4.3 us
    ppermute x1, waiting for transfers between devices, flip_z(): return lax.ppermute(a, 'row', [(i, i ^ bit) for i in range(nz)])  3.35 us
  transfers between devices with their start and end apart: 41, of which 26 were waited for; matrix products, arithmetic and copies ran while one was open for 0% of the time, Pallas kernels for 0%

profile of v2, /device:TPU:8, one launch (start us, length us, event | category | flops | bytes accessed | tf_op | source)
XLA Modules:
  0.0 154.7 jit_solution(5989838066972270989)
XLA Ops:
  2.6 4.0 %collective-permute-start = (bf16[32,2048]{1,0:T(8,128)(2,1)}, bf16[32,2048]{1,0:T(8,128)(2,1)S(1)}, u32[]{:S(2)}, u32[]{:S(2)}) collective-permute-start(bf16[32,2048]{1,0:T(8,128)(2,1)} %bitcast.14), channel_id=1, source_target_pairs={{0,224},{32,0},{64,32},{96,64},{128,96},{160,128},{192,160},{224,1... | collective-permute-start | bytes 393224 | tf_op jit(solution)/shard_map/ppermute | solution.py:326
  6.7 3.6 %collective-permute-done.3.refs_7_ = bf16[32,2048]{1,0:T(8,128)(2,1)S(1)} collective-permute-done((bf16[32,2048]{1,0:T(8,128)(2,1)}, bf16[32,2048]{1,0:T(8,128)(2,1)S(1)}, u32[]{:S(2)}, u32[]{:S(2)}) %collective-permute-start.3) | collective-permute-done | bytes 131104 | tf_op jit(solution)/shard_map/ppermute | solution.py:326
  10.3 3.2 %collective-permute-start.1 = (bf16[32,2048]{1,0:T(8,128)(2,1)S(1)}, bf16[32,2048]{1,0:T(8,128)(2,1)S(1)}, u32[]{:S(2)}, u32[]{:S(2)}) collective-permute-start(bf16[32,2048]{1,0:T(8,128)(2,1)S(1)} %collective-permute-done.refs_1_), channel_id=1, source_target_pairs={{0,224},{32,0},{64,32},{96,64},{128,96},{160,128},{192,160},{224,1... | collective-permute-start | bytes 393224 | tf_op jit(solution)/shard_map/ppermute | solution.py:326
  13.5 2.9 %collective-permute-done.4.refs_6_ = bf16[32,2048]{1,0:T(8,128)(2,1)S(1)} collective-permute-done((bf16[32,2048]{1,0:T(8,128)(2,1)S(1)}, bf16[32,2048]{1,0:T(8,128)(2,1)S(1)}, u32[]{:S(2)}, u32[]{:S(2)}) %collective-permute-start.4) | collective-permute-done | bytes 131104 | tf_op jit(solution)/shard_map/ppermute | solution.py:326
  16.5 3.2 %collective-permute-start.2 = (bf16[32,2048]{1,0:T(8,128)(2,1)S(1)}, bf16[32,2048]{1,0:T(8,128)(2,1)S(1)}, u32[]{:S(2)}, u32[]{:S(2)}) collective-permute-start(bf16[32,2048]{1,0:T(8,128)(2,1)S(1)} %collective-permute-done.1.refs_2_), channel_id=1, source_target_pairs={{0,224},{32,0},{64,32},{96,64},{128,96},{160,128},{192,160},{224,1... | collective-permute-start | bytes 393224 | tf_op jit(solution)/shard_map/ppermute | solution.py:326
  19.7 2.9 %collective-permute-done.5.refs_5_ = bf16[32,2048]{1,0:T(8,128)(2,1)S(1)} collective-permute-done((bf16[32,2048]{1,0:T(8,128)(2,1)S(1)}, bf16[32,2048]{1,0:T(8,128)(2,1)S(1)}, u32[]{:S(2)}, u32[]{:S(2)}) %collective-permute-start.5) | collective-permute-done | bytes 131104 | tf_op jit(solution)/shard_map/ppermute | solution.py:326
  24.4 4.4 %collective-permute-done.6.refs_4_ = bf16[32,2048]{1,0:T(8,128)(2,1)S(1)} collective-permute-done((bf16[32,2048]{1,0:T(8,128)(2,1)S(1)}, bf16[32,2048]{1,0:T(8,128)(2,1)S(1)}, u32[]{:S(2)}, u32[]{:S(2)}) %collective-permute-start.6) | collective-permute-done | bytes 131104 | tf_op jit(solution)/shard_map/ppermute | solution.py:326
  29.5 9.1 %shard_map.86 = (bf16[4,512,128]{2,1,0:T(8,128)(2,1)S(1)}, bf16[3,4,512,128]{3,2,1,0:T(8,128)(2,1)S(1)}, bf16[4,512,128]{2,1,0:T(8,128)(2,1)S(1)}, bf16[3,4,512,128]{3,2,1,0:T(8,128)(2,1)S(1)}) custom-call(s32[2,320]{1,0:T(2,128)S(1)} %bitcast.16, s32[1]{0:T(128)} %bitcast.11.count_ref, s32[4]{0:T(128)S(1)} %pad_add_fusion.at_ref, ...), custom_call_target="tpu_custom_call" | custom-call | flops 2684354560 | bytes 15731220 | tf_op jit(solution)/shard_map/pallas_call | solution.py:22
  44.2 4.3 %collective-permute-done.9.low = bf16[2,512,128]{2,1,0:T(8,128)(2,1)S(1)} collective-permute-done((bf16[2,512,128]{2,1,0:T(8,128)(2,1)S(1)}, bf16[2,512,128]{2,1,0:T(8,128)(2,1)S(1)}, u32[]{:S(2)}, u32[]{:S(2)}) %collective-permute-start.9) | collective-permute-done | bytes 262176 | tf_op jit(solution)/shard_map/ppermute | solution.py:320
  52.4 7.1 %collective-permute-done.11.minus = bf16[4,512,128]{2,1,0:T(8,128)(2,1)S(1)} collective-permute-done((bf16[4,512,128]{2,1,0:T(8,128)(2,1)S(1)}, bf16[4,512,128]{2,1,0:T(8,128)(2,1)S(1)}, u32[]{:S(2)}, u32[]{:S(2)}) %collective-permute-start.11) | collective-permute-done | bytes 524320 | tf_op jit(solution)/shard_map/ppermute | solution.py:320
  65.2 3.2 %collective-permute-done.14.c = bf16[512,128]{1,0:T(8,128)(2,1)S(1)} collective-permute-done((bf16[512,128]{1,0:T(8,128)(2,1)S(1)}, bf16[512,128]{1,0:T(8,128)(2,1)S(1)}, u32[]{:S(2)}, u32[]{:S(2)}) %collective-permute-start.14) | collective-permute-done | bytes 131104 | tf_op jit(solution)/shard_map/ppermute | solution.py:320
  85.4 7.2 %collective-permute-done.22.plus.refs_2_ = bf16[2112,128]{1,0:T(8,128)(2,1)S(1)} collective-permute-done((bf16[2112,128]{1,0:T(8,128)(2,1)S(1)}, bf16[2112,128]{1,0:T(8,128)(2,1)S(1)}, u32[]{:S(2)}, u32[]{:S(2)}) %collective-permute-start.22) | collective-permute-done | bytes 540704 | tf_op jit(solution)/shard_map/ppermute | solution.py:320
  92.6 3.4 %collective-permute-done.21.minus.refs_1_ = bf16[2112,128]{1,0:T(8,128)(2,1)S(1)} collective-permute-done((bf16[2112,128]{1,0:T(8,128)(2,1)S(1)}, bf16[2112,128]{1,0:T(8,128)(2,1)S(1)}, u32[]{:S(2)}, u32[]{:S(2)}) %collective-permute-start.21) | collective-permute-done | bytes 540704 | tf_op jit(solution)/shard_map/ppermute | solution.py:320
  96.3 3.2 %collective-permute-start.25 = (bf16[1024,128]{1,0:T(8,128)(2,1)S(1)}, bf16[1024,128]{1,0:T(8,128)(2,1)S(1)}, u32[]{:S(2)}, u32[]{:S(2)}) collective-permute-start(bf16[1024,128]{1,0:T(8,128)(2,1)S(1)} %get-tuple-element.72), channel_id=1, source_target_pairs={{0,24},{1,25},{2,26},{3,27},{4,7},{5,4},{6,5},{7,6},{8,0},{9,1},{1... | collective-permute-start | bytes 786440 | tf_op jit(solution)/shard_map/ppermute | solution.py:320
  99.5 4.5 %collective-permute-done.24.refs_3_ = bf16[1088,128]{1,0:T(8,128)(2,1)S(1)} collective-permute-done((bf16[1088,128]{1,0:T(8,128)(2,1)S(1)}, bf16[1088,128]{1,0:T(8,128)(2,1)S(1)}, u32[]{:S(2)}, u32[]{:S(2)}) %collective-permute-start.24) | collective-permute-done | bytes 278560 | tf_op jit(solution)/shard_map/ppermute | solution.py:320
  106.0 9.1 %shard_map.95 = (bf16[64,128]{1,0:T(8,128)(2,1)S(1)}, bf16[512,128]{1,0:T(8,128)(2,1)S(1)}, bf16[512,128]{1,0:T(8,128)(2,1)S(1)}, bf16[512,128]{1,0:T(8,128)(2,1...) custom-call(s32[2,320]{1,0:T(2,128)S(1)} %bitcast.17, ...), custom_call_target="tpu_custom_call" | custom-call | flops 2684354560 | bytes 15878676 | tf_op jit(solution)/shard_map/pallas_call | solution.py:22
  115.2 3.2 %collective-permute-start.30 = (bf16[576,128]{1,0:T(8,128)(2,1)S(1)}, bf16[576,128]{1,0:T(8,128)(2,1)S(1)}, u32[]{:S(2)}, u32[]{:S(2)}) collective-permute-start(bf16[576,128]{1,0:T(8,128)(2,1)S(1)} %get-tuple-element.77), channel_id=1, source_target_pairs={{0,224},{32,0},{64,32},{96,64},{128,96},{160,128},{192,160},{224,1... | collective-permute-start | bytes 442376 | tf_op jit(solution)/shard_map/ppermute | solution.py:326
  118.4 3.9 %collective-permute-done.29.up.refs_2_ = bf16[576,128]{1,0:T(8,128)(2,1)S(1)} collective-permute-done((bf16[576,128]{1,0:T(8,128)(2,1)S(1)}, bf16[576,128]{1,0:T(8,128)(2,1)S(1)}, u32[]{:S(2)}, u32[]{:S(2)}) %collective-permute-start.29) | collective-permute-done | bytes 147488 | tf_op jit(solution)/shard_map/ppermute | solution.py:326
  122.5 3.2 %collective-permute-start.32 = (bf16[576,128]{1,0:T(8,128)(2,1)S(1)}, bf16[576,128]{1,0:T(8,128)(2,1)S(1)}, u32[]{:S(2)}, u32[]{:S(2)}) collective-permute-start(bf16[576,128]{1,0:T(8,128)(2,1)S(1)} %get-tuple-element.81), channel_id=1, source_target_pairs={{0,224},{32,0},{64,32},{96,64},{128,96},{160,128},{192,160},{224,1... | collective-permute-start | bytes 442376 | tf_op jit(solution)/shard_map/ppermute | solution.py:326
  125.7 3.1 %collective-permute-done.31.up.refs_4_ = bf16[576,128]{1,0:T(8,128)(2,1)S(1)} collective-permute-done((bf16[576,128]{1,0:T(8,128)(2,1)S(1)}, bf16[576,128]{1,0:T(8,128)(2,1)S(1)}, u32[]{:S(2)}, u32[]{:S(2)}) %collective-permute-start.31) | collective-permute-done | bytes 147488 | tf_op jit(solution)/shard_map/ppermute | solution.py:326
  128.9 2.5 %collective-permute-start.33 = (bf16[576,128]{1,0:T(8,128)(2,1)S(1)}, bf16[576,128]{1,0:T(8,128)(2,1)S(1)}, u32[]{:S(2)}, u32[]{:S(2)}) collective-permute-start(bf16[576,128]{1,0:T(8,128)(2,1)S(1)} %get-tuple-element.83), channel_id=1, source_target_pairs={{0,32},{32,64},{64,96},{96,128},{128,160},{160,192},{192,224},{224... | collective-permute-start | bytes 442376 | tf_op jit(solution)/shard_map/ppermute | solution.py:326
  132.3 4.3 %collective-permute-start.35 = (bf16[64,128]{1,0:T(8,128)(2,1)S(1)}, bf16[64,128]{1,0:T(8,128)(2,1)S(1)}, u32[]{:S(2)}, u32[]{:S(2)}) collective-permute-start(bf16[64,128]{1,0:T(8,128)(2,1)S(1)} %get-tuple-element.87.refs_0_), channel_id=1, source_target_pairs={{0,128},{32,160},{64,192},{96,224},{128,0},{160,32},{192,64},{224,... | collective-permute-start | bytes 49160 | tf_op jit(solution)/shard_map/ppermute | solution.py:329
  136.6 3.3 %collective-permute-done.35.refs_1_ = bf16[64,128]{1,0:T(8,128)(2,1)S(1)} collective-permute-done((bf16[64,128]{1,0:T(8,128)(2,1)S(1)}, bf16[64,128]{1,0:T(8,128)(2,1)S(1)}, u32[]{:S(2)}, u32[]{:S(2)}) %collective-permute-start.35) | collective-permute-done | bytes 16416 | tf_op jit(solution)/shard_map/ppermute | solution.py:329
  143.3 3.6 %collective-permute-start.38 = (f32[64,128]{1,0:T(8,128)S(1)}, f32[64,128]{1,0:T(8,128)S(1)}, u32[]{:S(2)}, u32[]{:S(2)}) collective-permute-start(f32[64,128]{1,0:T(8,128)S(1)} %get-tuple-element.90.wa), channel_id=1, source_target_pairs={{0,2},{1,3},{2,0},{3,1},{4,20},{5,21},{6,22},{7,23},{8,10},{9,11},... | collective-permute-start | bytes 98312 | tf_op jit(solution)/shard_map/ppermute | solution.py:320
  (83 shorter events, 50.5 us)
Async XLA Ops:
  0.6 9.6 %collective-permute-start.3 = (bf16[32,2048]{1,0:T(8,128)(2,1)}, bf16[32,2048]{1,0:T(8,128)(2,1)S(1)}, u32[]{:S(2)}, u32[]{:S(2)}) collective-permute-start(bf16[32,2048]{1,0:T(8,128)(2,1)} %bitcast.13), channel_id=1, source_target_pairs={{0,32},{32,64},{64,96},{96,128},{128,160},{160,192},{192,224},{224... | collective-permute-start | bytes 393224 | tf_op jit(solution)/shard_map/ppermute | solution.py:326
  2.6 7.7 %collective-permute-start = (bf16[32,2048]{1,0:T(8,128)(2,1)}, bf16[32,2048]{1,0:T(8,128)(2,1)S(1)}, u32[]{:S(2)}, u32[]{:S(2)}) collective-permute-start(bf16[32,2048]{1,0:T(8,128)(2,1)} %bitcast.14), channel_id=1, source_target_pairs={{0,224},{32,0},{64,32},{96,64},{128,96},{160,128},{192,160},{224,1... | collective-permute-start | bytes 393224 | tf_op jit(solution)/shard_map/ppermute | solution.py:326
  16.5 8.0 %collective-permute-start.2 = (bf16[32,2048]{1,0:T(8,128)(2,1)S(1)}, bf16[32,2048]{1,0:T(8,128)(2,1)S(1)}, u32[]{:S(2)}, u32[]{:S(2)}) collective-permute-start(bf16[32,2048]{1,0:T(8,128)(2,1)S(1)} %collective-permute-done.1.refs_2_), channel_id=1, source_target_pairs={{0,224},{32,0},{64,32},{96,64},{128,96},{160,128},{192,160},{224,1... | collective-permute-start | bytes 393224 | tf_op jit(solution)/shard_map/ppermute | solution.py:326
  40.7 8.1 %collective-permute-start.8 = (bf16[3,4,512,128]{3,2,1,0:T(8,128)(2,1)S(1)}, bf16[3,4,512,128]{3,2,1,0:T(8,128)(2,1)S(1)}, u32[]{:S(2)}, u32[]{:S(2)}) collective-permute-start(bf16[3,4,512,128]{3,2,1,0:T(8,128)(2,1)S(1)} %get-tuple-element.52), channel_id=1, source_target_pairs={{0,4},{4,0},{8,12},{12,8},{16,20},{20,16},{24,28},{28,24},{1,5},{5... | collective-permute-start | bytes 4718600 | tf_op jit(solution)/shard_map/ppermute | solution.py:323
  40.9 7.6 %collective-permute-start.9 = (bf16[2,512,128]{2,1,0:T(8,128)(2,1)S(1)}, bf16[2,512,128]{2,1,0:T(8,128)(2,1)S(1)}, u32[]{:S(2)}, u32[]{:S(2)}) collective-permute-start(bf16[2,512,128]{2,1,0:T(8,128)(2,1)S(1)} %get-tuple-element.53), channel_id=1, source_target_pairs={{0,8},{1,9},{2,10},{3,11},{4,5},{5,6},{6,7},{7,4},{8,16},{9,17},{1... | collective-permute-start | bytes 786440 | tf_op jit(solution)/shard_map/ppermute | solution.py:320
  42.4 6.4 %collective-permute-start.10 = (bf16[2,512,128]{2,1,0:T(8,128)(2,1)S(1)}, bf16[2,512,128]{2,1,0:T(8,128)(2,1)S(1)}, u32[]{:S(2)}, u32[]{:S(2)}) collective-permute-start(bf16[2,512,128]{2,1,0:T(8,128)(2,1)S(1)} %get-tuple-element.54), channel_id=1, source_target_pairs={{0,24},{1,25},{2,26},{3,27},{4,7},{5,4},{6,5},{7,6},{8,0},{9,1},{1... | collective-permute-start | bytes 786440 | tf_op jit(solution)/shard_map/ppermute | solution.py:320
  49.1 10.5 %collective-permute-start.11 = (bf16[4,512,128]{2,1,0:T(8,128)(2,1)S(1)}, bf16[4,512,128]{2,1,0:T(8,128)(2,1)S(1)}, u32[]{:S(2)}, u32[]{:S(2)}) collective-permute-start(bf16[4,512,128]{2,1,0:T(8,128)(2,1)S(1)} %get-tuple-element.55), channel_id=1, source_target_pairs={{0,8},{1,9},{2,10},{3,11},{4,5},{5,6},{6,7},{7,4},{8,16},{9,17},{1... | collective-permute-start | bytes 1572872 | tf_op jit(solution)/shard_map/ppermute | solution.py:320
  50.7 9.2 %collective-permute-start.12 = (bf16[4,512,128]{2,1,0:T(8,128)(2,1)S(1)}, bf16[4,512,128]{2,1,0:T(8,128)(2,1)S(1)}, u32[]{:S(2)}, u32[]{:S(2)}) collective-permute-start(bf16[4,512,128]{2,1,0:T(8,128)(2,1)S(1)} %get-tuple-element.56), channel_id=1, source_target_pairs={{0,24},{1,25},{2,26},{3,27},{4,7},{5,4},{6,5},{7,6},{8,0},{9,1},{1... | collective-permute-start | bytes 1572872 | tf_op jit(solution)/shard_map/ppermute | solution.py:320
  61.8 6.6 %collective-permute-start.14 = (bf16[512,128]{1,0:T(8,128)(2,1)S(1)}, bf16[512,128]{1,0:T(8,128)(2,1)S(1)}, u32[]{:S(2)}, u32[]{:S(2)}) collective-permute-start(bf16[512,128]{1,0:T(8,128)(2,1)S(1)} %get-tuple-element.59), channel_id=1, source_target_pairs={{0,2},{1,3},{2,0},{3,1},{4,20},{5,21},{6,22},{7,23},{8,10},{9,11},... | collective-permute-start | bytes 393224 | tf_op jit(solution)/shard_map/ppermute | solution.py:320
  62.7 6.4 %collective-permute-start.15 = (bf16[512,128]{1,0:T(8,128)(2,1)S(1)}, bf16[512,128]{1,0:T(8,128)(2,1)S(1)}, u32[]{:S(2)}, u32[]{:S(2)}) collective-permute-start(bf16[512,128]{1,0:T(8,128)(2,1)S(1)} %get-tuple-element.60), channel_id=1, source_target_pairs={{0,3},{1,0},{2,1},{3,2},{4,28},{5,29},{6,30},{7,31},{8,11},{9,8},{... | collective-permute-start | bytes 393224 | tf_op jit(solution)/shard_map/ppermute | solution.py:320
  74.5 6.6 %collective-permute-start.19 = (bf16[576,128]{1,0:T(8,128)(2,1)S(1)}, bf16[576,128]{1,0:T(8,128)(2,1)S(1)}, u32[]{:S(2)}, u32[]{:S(2)}) collective-permute-start(bf16[576,128]{1,0:T(8,128)(2,1)S(1)} %get-tuple-element.69), channel_id=1, source_target_pairs={{0,2},{1,3},{2,0},{3,1},{4,20},{5,21},{6,22},{7,23},{8,10},{9,11},... | collective-permute-start | bytes 442376 | tf_op jit(solution)/shard_map/ppermute | solution.py:320
  83.3 9.4 %collective-permute-start.22 = (bf16[2112,128]{1,0:T(8,128)(2,1)S(1)}, bf16[2112,128]{1,0:T(8,128)(2,1)S(1)}, u32[]{:S(2)}, u32[]{:S(2)}) collective-permute-start(bf16[2112,128]{1,0:T(8,128)(2,1)S(1)} %shard_map.93.refs_0_), channel_id=1, source_target_pairs={{0,24},{1,25},{2,26},{3,27},{4,7},{5,4},{6,5},{7,6},{8,0},{9,1},{1... | collective-permute-start | bytes 1622024 | tf_op jit(solution)/shard_map/ppermute | solution.py:320
  85.4 10.6 %collective-permute-start.21 = (bf16[2112,128]{1,0:T(8,128)(2,1)S(1)}, bf16[2112,128]{1,0:T(8,128)(2,1)S(1)}, u32[]{:S(2)}, u32[]{:S(2)}) collective-permute-start(bf16[2112,128]{1,0:T(8,128)(2,1)S(1)} %shard_map.93.refs_0_), channel_id=1, source_target_pairs={{0,8},{1,9},{2,10},{3,11},{4,5},{5,6},{6,7},{7,4},{8,16},{9,17},{1... | collective-permute-start | bytes 1622024 | tf_op jit(solution)/shard_map/ppermute | solution.py:320
  96.1 9.9 %collective-permute-start.26 = (bf16[4096,128]{1,0:T(8,128)(2,1)S(1)}, bf16[4096,128]{1,0:T(8,128)(2,1)S(1)}, u32[]{:S(2)}, u32[]{:S(2)}) collective-permute-start(bf16[4096,128]{1,0:T(8,128)(2,1)S(1)} %get-tuple-element.74), channel_id=1, source_target_pairs={{0,4},{4,0},{8,12},{12,8},{16,20},{20,16},{24,28},{28,24},{1,5},{5... | collective-permute-start | bytes 3145736 | tf_op jit(solution)/shard_map/ppermute | solution.py:323
  96.2 7.8 %collective-permute-start.24 = (bf16[1088,128]{1,0:T(8,128)(2,1)S(1)}, bf16[1088,128]{1,0:T(8,128)(2,1)S(1)}, u32[]{:S(2)}, u32[]{:S(2)}) collective-permute-start(bf16[1088,128]{1,0:T(8,128)(2,1)S(1)} %get-tuple-element.71), channel_id=1, source_target_pairs={{0,8},{1,9},{2,10},{3,11},{4,5},{5,6},{6,7},{7,4},{8,16},{9,17},{1... | collective-permute-start | bytes 835592 | tf_op jit(solution)/shard_map/ppermute | solution.py:320
  96.3 7.8 %collective-permute-start.25 = (bf16[1024,128]{1,0:T(8,128)(2,1)S(1)}, bf16[1024,128]{1,0:T(8,128)(2,1)S(1)}, u32[]{:S(2)}, u32[]{:S(2)}) collective-permute-start(bf16[1024,128]{1,0:T(8,128)(2,1)S(1)} %get-tuple-element.72), channel_id=1, source_target_pairs={{0,24},{1,25},{2,26},{3,27},{4,7},{5,4},{6,5},{7,6},{8,0},{9,1},{1... | collective-permute-start | bytes 786440 | tf_op jit(solution)/shard_map/ppermute | solution.py:320
  115.1 7.2 %collective-permute-start.29 = (bf16[576,128]{1,0:T(8,128)(2,1)S(1)}, bf16[576,128]{1,0:T(8,128)(2,1)S(1)}, u32[]{:S(2)}, u32[]{:S(2)}) collective-permute-start(bf16[576,128]{1,0:T(8,128)(2,1)S(1)} %get-tuple-element.75), channel_id=1, source_target_pairs={{0,32},{32,64},{64,96},{96,128},{128,160},{160,192},{192,224},{224... | collective-permute-start | bytes 442376 | tf_op jit(solution)/shard_map/ppermute | solution.py:326
  115.2 7.1 %collective-permute-start.30 = (bf16[576,128]{1,0:T(8,128)(2,1)S(1)}, bf16[576,128]{1,0:T(8,128)(2,1)S(1)}, u32[]{:S(2)}, u32[]{:S(2)}) collective-permute-start(bf16[576,128]{1,0:T(8,128)(2,1)S(1)} %get-tuple-element.77), channel_id=1, source_target_pairs={{0,224},{32,0},{64,32},{96,64},{128,96},{160,128},{192,160},{224,1... | collective-permute-start | bytes 442376 | tf_op jit(solution)/shard_map/ppermute | solution.py:326
  122.4 6.4 %collective-permute-start.31 = (bf16[576,128]{1,0:T(8,128)(2,1)S(1)}, bf16[576,128]{1,0:T(8,128)(2,1)S(1)}, u32[]{:S(2)}, u32[]{:S(2)}) collective-permute-start(bf16[576,128]{1,0:T(8,128)(2,1)S(1)} %get-tuple-element.79), channel_id=1, source_target_pairs={{0,32},{32,64},{64,96},{96,128},{128,160},{160,192},{192,224},{224... | collective-permute-start | bytes 442376 | tf_op jit(solution)/shard_map/ppermute | solution.py:326
  122.5 6.3 %collective-permute-start.32 = (bf16[576,128]{1,0:T(8,128)(2,1)S(1)}, bf16[576,128]{1,0:T(8,128)(2,1)S(1)}, u32[]{:S(2)}, u32[]{:S(2)}) collective-permute-start(bf16[576,128]{1,0:T(8,128)(2,1)S(1)} %get-tuple-element.81), channel_id=1, source_target_pairs={{0,224},{32,0},{64,32},{96,64},{128,96},{160,128},{192,160},{224,1... | collective-permute-start | bytes 442376 | tf_op jit(solution)/shard_map/ppermute | solution.py:326
  128.9 11.0 %collective-permute-start.33 = (bf16[576,128]{1,0:T(8,128)(2,1)S(1)}, bf16[576,128]{1,0:T(8,128)(2,1)S(1)}, u32[]{:S(2)}, u32[]{:S(2)}) collective-permute-start(bf16[576,128]{1,0:T(8,128)(2,1)S(1)} %get-tuple-element.83), channel_id=1, source_target_pairs={{0,32},{32,64},{64,96},{96,128},{128,160},{160,192},{192,224},{224... | collective-permute-start | bytes 442376 | tf_op jit(solution)/shard_map/ppermute | solution.py:326
  131.4 8.5 %collective-permute-start.34 = (bf16[576,128]{1,0:T(8,128)(2,1)S(1)}, bf16[576,128]{1,0:T(8,128)(2,1)S(1)}, u32[]{:S(2)}, u32[]{:S(2)}) collective-permute-start(bf16[576,128]{1,0:T(8,128)(2,1)S(1)} %get-tuple-element.85), channel_id=1, source_target_pairs={{0,224},{32,0},{64,32},{96,64},{128,96},{160,128},{192,160},{224,1... | collective-permute-start | bytes 442376 | tf_op jit(solution)/shard_map/ppermute | solution.py:326
  132.3 7.6 %collective-permute-start.35 = (bf16[64,128]{1,0:T(8,128)(2,1)S(1)}, bf16[64,128]{1,0:T(8,128)(2,1)S(1)}, u32[]{:S(2)}, u32[]{:S(2)}) collective-permute-start(bf16[64,128]{1,0:T(8,128)(2,1)S(1)} %get-tuple-element.87.refs_0_), channel_id=1, source_target_pairs={{0,128},{32,160},{64,192},{96,224},{128,0},{160,32},{192,64},{224,... | collective-permute-start | bytes 49160 | tf_op jit(solution)/shard_map/ppermute | solution.py:329
  140.6 10.2 %collective-permute-start.36 = (bf16[512,128]{1,0:T(8,128)(2,1)S(1)}, bf16[512,128]{1,0:T(8,128)(2,1)S(1)}, u32[]{:S(2)}, u32[]{:S(2)}) collective-permute-start(bf16[512,128]{1,0:T(8,128)(2,1)S(1)} %get-tuple-element.88), channel_id=1, source_target_pairs={{0,32},{32,64},{64,96},{96,128},{128,160},{160,192},{192,224},{224... | collective-permute-start | bytes 393224 | tf_op jit(solution)/shard_map/ppermute | solution.py:326
  (21 other events, 110.8 us)
